TPU v7x, 128 devices: a whole 4x4x4 slice. The times are simulated.
128 devices in a mesh: dp: 8 (over x, core), mp: 16 (over y, z).
Axes of the slice: x: 4, y: 4, z: 4, core: 2. Of those that a mesh axis runs over, the one named last changes fastest.
Arguments:
- patches: bfloat16 [3072, 6144], P('dp', 'mp'), may hold values from -6 to 6
- keep_index: int32 [64, 48], P('dp'), may hold values from 0 to 47, each once within a row
- keep_count: int32 [64], replicated, may hold values from 1 to 48, as said below
- pack_dest: int32 [64], replicated, may hold values from 0 to 7, as said below
- pack_offset: int32 [64], replicated, may hold values from 0 to 336, as said below
- w_qkv: bfloat16 [6144, 12288], P(None, 'mp'), may hold values from -0.108253175 to 0.108253175
- q_gain: float32 [128], replicated, may hold values from 0.6 to 5
- k_gain: float32 [128], replicated, may hold values from 0.6 to 5
- w_out: bfloat16 [6144, 4096], P(None, 'mp'), may hold values from -0.09375 to 0.09375
- cotangent: bfloat16 [3072, 6144], P('dp', 'mp'), may hold values from -6 to 6
Outputs:
- block_out: bfloat16 [3072, 6144], P('dp', 'mp')
- patch_grad: bfloat16 [3072, 6144], P('dp', 'mp')
- qkv_grad: float32 [6144, 12288], P('dp', 'mp')
- out_grad: float32 [6144, 4096], P('dp', 'mp')
Inputs may be any that keep to these rules, and one draw needn't show every extreme that they name: `pack_dest`: the 8 images s*8 to s*8 + 7 of loader shard s go to 8 different sequences, so every sequence receives exactly one image from each shard. `keep_count`: in every draw all images of some sequence keep all 48 slots. `pack_offset`: the images of one sequence lie back to back from row 0, in some order of their shards; rows after them are padding.
All inputs are finite; a program needn't handle non-finite values.
Results may differ from a plain program's by a relative error of at most 0.02.
The roundings to bfloat16 on the way count: a program that leaves them out, or rounds other values in their place, can miss the bound.
Values may be sent and summed in bfloat16 or wider, within the bound.
A program may use at most 128 MiB of HBM per device.

v0:
```python
import jax
import jax.numpy as jnp
from jax import lax
from jax.sharding import PartitionSpec as P

HEAD_DIM = 128


EPSILON = 1e-06


def head_norm(values, gain):
    row_mean = jnp.mean(values, axis=-1, keepdims=True)
    centred = values - row_mean
    variance = jnp.mean(centred * centred, axis=-1, keepdims=True)
    inverse = lax.rsqrt(variance + EPSILON)
    normed = centred * inverse
    return (normed * gain, normed, inverse)


def head_norm_back(incoming, normed, inverse, gain):
    scaled = incoming * gain
    return (
        scaled
        - jnp.mean(scaled, axis=-1, keepdims=True)
        - normed * jnp.mean(scaled * normed, axis=-1, keepdims=True)
    ) * inverse


def batched(form, left, right):
    return jnp.einsum(form, left, right, preferred_element_type=jnp.float32)


def attention_pass(projected, segment, q_gain, k_gain, grad_attended):
    row_count = projected.shape[0]
    head_count = projected.shape[1]
    head_size = projected.shape[3]
    queries = jnp.swapaxes(projected[:, :, 0, :], 0, 1).astype(jnp.float32)
    keys_raw = jnp.swapaxes(projected[:, :, 1, :], 0, 1).astype(jnp.float32)
    values = jnp.swapaxes(projected[:, :, 2, :], 0, 1)
    query_n, query_hat, query_inv = head_norm(queries, q_gain)
    key_n, key_hat, key_inv = head_norm(keys_raw, k_gain)
    query_b = query_n.astype(jnp.bfloat16)
    key_b = key_n.astype(jnp.bfloat16)
    score_scale = head_size ** (-0.5)
    scores = batched("htd,hsd->hts", query_b, key_b) * score_scale
    allowed = segment[:, None] == segment[None, :]
    scores = jnp.where(allowed[None], scores, -jnp.inf)
    largest = jnp.max(scores, axis=-1, keepdims=True)
    exponent = jnp.exp(scores - largest)
    probs = exponent / jnp.sum(exponent, axis=-1, keepdims=True)
    probs_b = probs.astype(jnp.bfloat16)
    attended = batched("hts,hsd->htd", probs_b, values).astype(jnp.bfloat16)
    attended = jnp.swapaxes(attended, 0, 1).reshape(row_count, head_count * head_size)
    grad_heads = jnp.swapaxes(grad_attended.reshape(row_count, head_count, head_size), 0, 1)
    grad_value = batched("hts,htd->hsd", probs_b, grad_heads).astype(jnp.bfloat16)
    grad_probs = batched("htd,hsd->hts", grad_heads, values)
    grad_scores = (
        probs * (grad_probs - jnp.sum(probs * grad_probs, axis=-1, keepdims=True)) * score_scale
    ).astype(jnp.bfloat16)
    grad_qn = batched("hts,hsd->htd", grad_scores, key_b)
    grad_kn = batched("hts,htd->hsd", grad_scores, query_b)
    grad_query = head_norm_back(grad_qn, query_hat, query_inv, q_gain).astype(jnp.bfloat16)
    grad_key = head_norm_back(grad_kn, key_hat, key_inv, k_gain).astype(jnp.bfloat16)
    stacked = jnp.stack([grad_query, grad_key, grad_value], axis=2)
    grad_proj = jnp.transpose(stacked, (1, 0, 2, 3)).reshape(row_count, head_count * 3 * head_size)
    return (attended, grad_proj)


def widen(local_rows):
    return lax.all_gather(local_rows, "mp", axis=1, tiled=True)


def reduce_features(term):
    return lax.psum_scatter(
        term.astype(jnp.bfloat16), "mp", scatter_dimension=1, tiled=True
    ).astype(jnp.float32)


def contract_rows(left, right):
    return lax.dot_general(
        left, right, (((0,), (0,)), ((), ())), preferred_element_type=jnp.float32
    )


def contract_columns(left, right):
    return lax.dot_general(
        left, right, (((1,), (1,)), ((), ())), preferred_element_type=jnp.float32
    )


def shards(
    patches, keep_index, keep_count, pack_dest, pack_offset, w_qkv, q_gain, k_gain, w_out, cotangent
):
    n_dp = lax.axis_size("dp")
    shard_index = lax.axis_index("dp")
    seq_rows = patches.shape[0]
    slots = seq_rows // n_dp
    width_dev = patches.shape[1]
    places = jnp.arange(n_dp, dtype=jnp.int32)
    slot_lanes = jnp.arange(slots, dtype=jnp.int32)
    dest_table = pack_dest.reshape(n_dp, n_dp)
    count_table = keep_count.reshape(n_dp, n_dp)
    my_dest = jnp.take(dest_table, shard_index, axis=0)
    my_count = jnp.take(count_table, shard_index, axis=0)
    chosen = jnp.sum(jnp.where(my_dest[None, :] == places[:, None], places[None, :], 0), axis=1)
    send_count = jnp.take(my_count, chosen)
    send_rows = chosen[:, None] * slots + jnp.take(keep_index, chosen, axis=0)
    send_live = slot_lanes[None, :] < send_count[:, None]
    taken = jnp.take(patches, send_rows.reshape(-1), axis=0).reshape(n_dp, slots, width_dev)
    outgoing = jnp.where(send_live[:, :, None], taken, jnp.zeros_like(taken))
    arrived = lax.all_to_all(outgoing, "dp", split_axis=0, concat_axis=0, tiled=True)
    from_shard = jnp.sum(jnp.where(dest_table == shard_index, places[None, :], 0), axis=1)
    image_ids = places * n_dp + from_shard
    recv_count = jnp.take(keep_count, image_ids)
    recv_offset = jnp.take(pack_offset, image_ids)
    positions = jnp.arange(seq_rows, dtype=jnp.int32)
    inside = (positions[:, None] >= recv_offset[None, :]) & (
        positions[:, None] < (recv_offset + recv_count)[None, :]
    )
    owner = jnp.sum(jnp.where(inside, places[None, :], 0), axis=1)
    present = jnp.any(inside, axis=1)
    local_row = positions - jnp.take(recv_offset, owner)
    flat_index = jnp.where(present, owner * slots + local_row, 0)
    gathered_rows = jnp.take(arrived.reshape(n_dp * slots, width_dev), flat_index, axis=0)
    packed = jnp.where(present[:, None], gathered_rows, jnp.zeros_like(gathered_rows))
    segment = jnp.where(present, jnp.take(image_ids, owner), -1)
    x_full = widen(packed)
    projected = jnp.dot(x_full, w_qkv, preferred_element_type=jnp.float32).astype(jnp.bfloat16)
    heads_dev = w_out.shape[1] // HEAD_DIM
    grad_rows = jnp.where(present[:, None], cotangent, jnp.zeros_like(cotangent))
    grad_full = widen(grad_rows)
    grad_attended = jnp.dot(grad_full, w_out, preferred_element_type=jnp.float32).astype(
        jnp.bfloat16
    )
    attended, grad_proj = attention_pass(
        projected.reshape(seq_rows, heads_dev, 3, HEAD_DIM), segment, q_gain, k_gain, grad_attended
    )
    proj_sum = reduce_features(contract_columns(attended, w_out))
    block_out = jnp.where(present[:, None], packed.astype(jnp.float32) + proj_sum, 0.0).astype(
        jnp.bfloat16
    )
    back_sum = reduce_features(contract_columns(grad_proj, w_qkv))
    grad_packed = (grad_rows.astype(jnp.float32) + back_sum).astype(jnp.bfloat16)
    back_rows = jnp.clip(recv_offset[:, None] + slot_lanes[None, :], 0, seq_rows - 1)
    back_live = slot_lanes[None, :] < recv_count[:, None]
    back_taken = jnp.take(grad_packed, back_rows.reshape(-1), axis=0).reshape(
        n_dp, slots, width_dev
    )
    outgoing_grad = jnp.where(back_live[:, :, None], back_taken, jnp.zeros_like(back_taken))
    returned = lax.all_to_all(outgoing_grad, "dp", split_axis=0, concat_axis=0, tiled=True)
    ranking = jnp.sum(
        jnp.where(
            keep_index[:, :, None] == slot_lanes[None, None, :], slot_lanes[None, :, None], 0
        ),
        axis=1,
    )
    kept = ranking < my_count[:, None]
    pick = my_dest[:, None] * slots + ranking
    picked = jnp.take(returned.reshape(n_dp * slots, width_dev), pick.reshape(-1), axis=0).reshape(
        n_dp, slots, width_dev
    )
    patch_grad = jnp.where(kept[:, :, None], picked, jnp.zeros_like(picked)).reshape(
        seq_rows, width_dev
    )
    qkv_part = contract_rows(x_full, grad_proj)
    out_part = contract_rows(grad_full, attended)
    qkv_grad, out_grad = (
        lax.psum_scatter(
            qkv_part.astype(jnp.bfloat16), "dp", scatter_dimension=0, tiled=True
        ).astype(jnp.float32),
        lax.psum_scatter(
            out_part.astype(jnp.bfloat16), "dp", scatter_dimension=0, tiled=True
        ).astype(jnp.float32),
    )
    return (block_out, patch_grad, qkv_grad, out_grad)


def solution(mesh):
    placed = (
        P("dp", "mp"),
        P("dp", None),
        P(),
        P(),
        P(),
        P(None, "mp"),
        P(),
        P(),
        P(None, "mp"),
        P("dp", "mp"),
    )
    return jax.shard_map(
        shards,
        mesh=mesh,
        in_specs=placed,
        out_specs=(P("dp", "mp"), P("dp", "mp"), P("dp", "mp"), P("dp", "mp")),
        check_vma=False,
    )
```

profile of v0, /device:TPU:1, one launch (start us, length us, event | category | flops | bytes accessed | tf_op | source)
XLA Modules:
  0.0 472.3 jit_solution(17536851693428514325)
XLA Ops:
  11.8 2.5 gather_fusion.4
  16.3 5.8 %all-to-all-start = ((bf16[8,48,384]{2,1,0:T(8,128)(2,1)}), bf16[8,48,384]{2,1,0:T(8,128)(2,1)S(1)}, u32[]{:S(2)}, u32[]{:S(2)}) async-start(bf16[8,48,384]{2,1,0:T(8,128)(2,1)} %broadcast_select_fusion.4), calls=%async_computation | async-start | bytes 589824 | tf_op jit(solution)/shard_map/all_to_all | solution.py:112
  24.8 5.1 %compare_and_fusion.2 = (pred[384]{0:T(512)(128)(4,1)S(1)}, s32[384]{0:T(512)S(1)}) fusion(pred[384]{0:T(512)(128)(4,1)S(1)} %fusion.49, s32[]{:T(128)} %bitcast.7, s32[]{:T(128)} %bitcast.6, s32[]{:T(128)} %bitcast.5, s32[]{:T(128)} %bitcast.4, s32[]{:T(128)} %bitcast.3, s32[]{:T(128)} %bitcast.2, s32[]{:T(128)} %bitcast.1, s32[]{:T(128)} %bitcast, ...), kind=kLoop, calls=%fused_computation.119 | loop fusion | flops 11904 | bytes 3872 | tf_op jit(solution)/shard_map/jit(_take)/and | solution.py:125
  29.9 2.5 gather_fusion.5
  32.4 2.1 broadcast_select_fusion.2
  36.1 5.0 %select_select_fusion.2 = s32[384]{0:T(512)S(1)} fusion(pred[384]{0:T(512)(128)(4,1)S(1)} %fusion.49, s32[]{:T(128)} %bitcast.21, s32[]{:T(128)} %bitcast.20, s32[]{:T(128)} %bitcast.19, s32[]{:T(128)} %bitcast.18, s32[]{:T(128)} %bitcast.17, s32[]{:T(128)} %bitcast.16, s32[]{:T(128)} %bitcast.15, s32[]{:T(128)} %bitcast.14, s32[384]{0:T(512)S(1)} %select_reduce_fusion.1), kind=kLoop, calls=%fused_computation.111 | loop fusion | flops 8448 | bytes 3488 | tf_op jit(solution)/shard_map/jit(_where)/select_n | solution.py:127
  41.3 55.0 %all-gather.3.cloned.1.call-done = bf16[384,6144]{1,0:T(8,128)(2,1)} async-done(((bf16[384,384]{1,0:T(8,128)(2,1)}), bf16[384,6144]{1,0:T(8,128)(2,1)}) %all-gather.3.cloned.1.call-update) | async-done | bytes 4718608 | tf_op jit(solution)/shard_map/all_gather | solution.py:71
  96.2 9.7 %convolution_convert_fusion.4 = bf16[384,768]{1,0:T(8,128)(2,1)} fusion(bf16[384,6144]{1,0:T(8,128)(2,1)} %all-gather.3.cloned.1.call-done, bf16[6144,768]{1,0:T(8,128)(2,1)} %param.23), kind=kOutput, calls=%fused_computation.22 | convolution fusion | flops 3624173568 | bytes 14745600 | tf_op jit(solution)/shard_map/dot_general | solution.py:129
  106.0 2.1 copy.51
  110.5 48.0 %all-gather.5.cloned.1.call-done = bf16[384,6144]{1,0:T(8,128)(2,1)} async-done(((bf16[384,384]{1,0:T(8,128)(2,1)}), bf16[384,6144]{1,0:T(8,128)(2,1)}) %all-gather.5.cloned.1.call-update) | async-done | bytes 4718608 | tf_op jit(solution)/shard_map/all_gather | solution.py:71
  158.4 4.2 convolution_convert_fusion.7
  162.6 2.4 fusion.47
  165.0 2.7 fusion.74
  168.3 2.3 fusion.9
  170.6 3.1 convolution_multiply_fusion.2
  173.8 4.6 fusion.38
  183.5 14.6 %convolution_convert_fusion.1 = bf16[384,6144]{1,0:T(8,128)(2,1)} fusion(bf16[384,768]{0,1:T(8,128)(2,1)S(1)} %bitcast.205, bf16[6144,768]{1,0:T(8,128)(2,1)} %param.23), kind=kOutput, calls=%fused_computation.11 | convolution fusion | flops 3626237952 | bytes 14745600 | tf_op jit(solution)/shard_map/dot_general | solution.py:87
  198.2 6.7 %copy.74 = bf16[384,6144]{0,1:T(8,128)(2,1)} copy(bf16[384,6144]{1,0:T(8,128)(2,1)} %convolution_convert_fusion.1) | data formatting | bytes 9437184
  207.2 5.9 %convolution_convert_fusion.3 = bf16[6144,256]{1,0:T(8,128)(2,1)} fusion(bf16[384,6144]{1,0:T(8,128)(2,1)} %all-gather.5.cloned.1.call-done, bf16[384,256]{0,1:T(8,128)(2,1)S(1)} %bitcast.203), kind=kOutput, calls=%fused_computation.13 | convolution fusion | flops 1209532416 | bytes 8060928 | tf_op jit(solution)/shard_map/dot_general | solution.py:81
  213.2 3.6 convolution_convert_fusion.2
  216.8 6.6 %copy.72 = bf16[384,6144]{0,1:T(8,128)(2,1)} copy(bf16[384,6144]{1,0:T(8,128)(2,1)} %convolution_convert_fusion.2) | data formatting | bytes 9437184
  223.5 9.3 %convolution_convert_fusion = bf16[6144,768]{1,0:T(8,128)(2,1)} fusion(bf16[384,6144]{1,0:T(8,128)(2,1)} %all-gather.3.cloned.1.call-done, bf16[384,768]{0,1:T(8,128)(2,1)} %bitcast.206), kind=kOutput, calls=%fused_computation.10 | convolution fusion | flops 3628597248 | bytes 14745600 | tf_op jit(solution)/shard_map/dot_general | solution.py:81
  234.1 48.1 %reduce-scatter.15.cloned.1.call-done = bf16[384,384]{1,0:T(8,128)(2,1)} async-done(((bf16[6144,384]{1,0:T(8,128)(2,1)}), bf16[384,384]{1,0:T(8,128)(2,1)}) %reduce-scatter.15.cloned.1.call-update) | async-done | bytes 294928
  285.2 2.5 gather_fusion.6
  289.6 6.7 %all-to-all-start.1 = ((bf16[8,48,384]{2,1,0:T(8,128)(2,1)}), bf16[8,48,384]{2,1,0:T(8,128)(2,1)S(1)}, u32[]{:S(2)}, u32[]{:S(2)}) async-start(bf16[8,48,384]{2,1,0:T(8,128)(2,1)} %broadcast_select_fusion.3), calls=%async_computation.1 | async-start | bytes 589824 | tf_op jit(solution)/shard_map/all_to_all | solution.py:151
  296.4 23.8 %reduce-scatter.11.cloned.1.call-done = bf16[768,256]{1,0:T(8,128)(2,1)} async-done(((bf16[6144,256]{1,0:T(8,128)(2,1)}), bf16[768,256]{1,0:T(8,128)(2,1)}) %reduce-scatter.11.cloned.1.call-update) | async-done | bytes 393232 | tf_op jit(solution)/shard_map/reduce_scatter | solution.py:172
  320.1 1.9 convert_element_type.116
  322.1 80.6 %reduce-scatter.13.cloned.1.call-done = bf16[384,384]{1,0:T(8,128)(2,1)} async-done(((bf16[6144,384]{1,0:T(8,128)(2,1)}), bf16[384,384]{1,0:T(8,128)(2,1)}) %reduce-scatter.13.cloned.1.call-update) | async-done | bytes 294928
  404.5 1.9 select_convert_fusion
  406.4 2.5 gather_fusion.7
  410.8 51.8 %reduce-scatter.9.cloned.1.call-done = bf16[768,768]{1,0:T(8,128)(2,1)} async-done(((bf16[6144,768]{1,0:T(8,128)(2,1)}), bf16[768,768]{1,0:T(8,128)(2,1)}) %reduce-scatter.9.cloned.1.call-update) | async-done | bytes 1179664 | tf_op jit(solution)/shard_map/reduce_scatter | solution.py:169
  462.6 2.8 convert_element_type.114
  (111 shorter events, 31.4 us)
Async XLA Ops:
  7.2 151.3 %copy-start = (bf16[6144,256]{1,0:T(8,128)(2,1)S(1)}, bf16[6144,256]{1,0:T(8,128)(2,1)}, u32[]{:S(2)}) copy-start(bf16[6144,256]{1,0:T(8,128)(2,1)} %param.26) | copy-start | bytes 9437188
  7.2 4.6 copy-start.3
  14.3 7.8 %copy-start.1 = (s32[64]{0:T(128)S(1)}, s32[64]{0:T(128)}, u32[]{:S(2)}) copy-start(s32[64]{0:T(128)} %param.20) | copy-start | bytes 772
  14.3 8.4 %copy-start.2 = (s32[64]{0:T(128)S(1)}, s32[64]{0:T(128)}, u32[]{:S(2)}) copy-start(s32[64]{0:T(128)} %param.22) | copy-start | bytes 772
  16.3 13.6 %all-to-all-start = ((bf16[8,48,384]{2,1,0:T(8,128)(2,1)}), bf16[8,48,384]{2,1,0:T(8,128)(2,1)S(1)}, u32[]{:S(2)}, u32[]{:S(2)}) async-start(bf16[8,48,384]{2,1,0:T(8,128)(2,1)} %broadcast_select_fusion.4), calls=%async_computation | async-start | bytes 589824 | tf_op jit(solution)/shard_map/all_to_all | solution.py:112
  22.1 74.2 %all-gather.3.cloned.1.call-start = ((), (), s32[]{:S(2)}) async-start(), calls=%async_computation.6 | async-start | bytes 5013504 | tf_op jit(solution)/shard_map/all_gather | solution.py:71
  24.0 12.1 %copy-start.9 = (pred[384]{0:T(512)(128)(4,1)}, pred[384]{0:T(512)(128)(4,1)S(1)}, u32[]{:S(2)}) copy-start(pred[384]{0:T(512)(128)(4,1)S(1)} %fusion.49) | copy-start | bytes 1156
  34.5 123.9 %all-gather.5.cloned.1.call-start = ((), (), s32[]{:S(2)}) async-start(), calls=%async_computation.7 | async-start | bytes 5013504 | tf_op jit(solution)/shard_map/all_gather | solution.py:71
  35.2 246.9 %reduce-scatter.15.cloned.1.call-start = ((), (), s32[]{:S(2)}) async-start(), calls=%async_computation.11 | async-start | bytes 5013504
  110.4 54.6 %copy-start.7 = (f32[2,384]{1,0:T(2,128)}, f32[2,384]{1,0:T(2,128)S(1)}, u32[]{:S(2)}) copy-start(f32[2,384]{1,0:T(2,128)S(1)} %add_rsqrt_fusion) | copy-start | bytes 9220
  110.5 54.5 %copy-start.8 = (f32[2,384]{1,0:T(2,128)}, f32[2,384]{1,0:T(2,128)S(1)}, u32[]{:S(2)}) copy-start(f32[2,384]{1,0:T(2,128)S(1)} %add_rsqrt_fusion.1) | copy-start | bytes 9220
  162.6 2.4 copy-start.13
  162.6 2.4 copy-start.14
  167.7 0.6 copy-start.15
  178.4 4.1 copy-start.6
  182.7 0.8 copy-start.4
  204.9 0.7 copy-start.16
  204.9 115.3 %reduce-scatter.11.cloned.1.call-start = ((), (), s32[]{:S(2)}) async-start(), calls=%async_computation.9 | async-start | bytes 3538944 | tf_op jit(solution)/shard_map/reduce_scatter | solution.py:172
  213.1 189.5 %reduce-scatter.13.cloned.1.call-start = ((), (), s32[]{:S(2)}) async-start(), calls=%async_computation.10 | async-start | bytes 5013504
  223.4 239.2 %reduce-scatter.9.cloned.1.call-start = ((), (), s32[]{:S(2)}) async-start(), calls=%async_computation.8 | async-start | bytes 10616832 | tf_op jit(solution)/shard_map/reduce_scatter | solution.py:169
  232.8 0.7 copy-start.5
  232.8 0.8 copy-start.11
  232.8 1.2 copy-start.12
  289.6 114.9 %copy-start.10 = (pred[384]{0:T(512)(128)(4,1)S(1)}, pred[384]{0:T(512)(128)(4,1)}, u32[]{:S(2)}) copy-start(pred[384]{0:T(512)(128)(4,1)} %copy-done.9) | copy-start | bytes 1156
  289.6 116.8 %all-to-all-start.1 = ((bf16[8,48,384]{2,1,0:T(8,128)(2,1)}), bf16[8,48,384]{2,1,0:T(8,128)(2,1)S(1)}, u32[]{:S(2)}, u32[]{:S(2)}) async-start(bf16[8,48,384]{2,1,0:T(8,128)(2,1)} %broadcast_select_fusion.3), calls=%async_computation.1 | async-start | bytes 589824 | tf_op jit(solution)/shard_map/all_to_all | solution.py:151
Sparse Core Ops, SparseCore 0:
  34.6 61.5 all-gather.2
  98.9 59.4 all-gather.4
  205.0 77.1 reduce-scatter.14
  284.5 35.6 reduce-scatter.10
  323.3 79.2 reduce-scatter.12
  404.9 57.6 reduce-scatter.8
where the time goes:
time: 474 us; the launch traced here: 472 us
  waiting for transfers between devices  308 us (65%)
  matrix products  64.1 us (14%)
  local copies, waits for them, and re-layouts  38.3 us (8%)
  other arithmetic  34.4 us (7%)
  between operations  14.4 us (3%)
  starting transfers between devices  13.1 us (3%)
    unnamed x8, waiting for transfers between devices  129 us
    all_gather x2, waiting for transfers between devices, widen(): return lax.all_gather(local_rows, 'mp', axis=1, tiled=True)  103 us
    reduce_scatter x1, waiting for transfers between devices, shards(): lax.psum_scatter(qkv_part.astype(jnp.bfloat16), 'dp', scatter_dimension=0...  51.8 us
    reduce_scatter x1, waiting for transfers between devices, shards(): lax.psum_scatter(out_part.astype(jnp.bfloat16), 'dp', scatter_dimension=0...  23.8 us
    unnamed x38, local copies, waits for them, and re-layouts  19.5 us
    dot_general x2, matrix products, contract_columns(): lax.dot_general(left, right, (((1,), (1,)), ((), ())), preferred_element_...  18.2 us
    dot_general x2, matrix products, contract_rows(): lax.dot_general(left, right, (((0,), (0,)), ((), ())), preferred_element_...  15.2 us
    dot_general x5, matrix products, batched(): return jnp.einsum(form, left, right, preferred_element_type=jnp.float32)  14.1 us
  transfers between devices with their start and end apart: 8, of which 6 were waited for; matrix products, arithmetic and copies ran while one was open for 15% of the time, Pallas kernels for 0%

commit v1 on v0

v1 whole, which is shorter than its diff:
```python
import functools

import jax
import jax.numpy as jnp
from jax import lax
from jax.experimental import pallas as pl
from jax.experimental.pallas import tpu as pltpu
from jax.sharding import PartitionSpec as P

MESH = pl.DeviceIdType.MESH
BF, F32 = jnp.bfloat16, jnp.float32
N_DP, RING = 8, 4
ROWS = 384
SLOTS = 48
FEAT = 384
D = 6144
HEAD = 128
HEADS_DEV = 2
QKV = 3 * HEAD * HEADS_DEV
OUT = HEAD * HEADS_DEV
GRAD_ROWS = D // N_DP
HALF, QUART = ROWS // 2, ROWS // 4
EPSILON = 1e-06
SCALE = HEAD ** (-0.5)
N_SEMS = 256


def dot(a, b):
    return jnp.dot(a, b, preferred_element_type=F32)


def dot_nt(a, b):
    return lax.dot_general(a, b, (((1,), (1,)), ((), ())), preferred_element_type=F32)


def dot_tn(a, b):
    return lax.dot_general(a, b, (((0,), (0,)), ((), ())), preferred_element_type=F32)


def head_norm(values):
    centred = values - jnp.mean(values, axis=-1, keepdims=True)
    variance = jnp.mean(centred * centred, axis=-1, keepdims=True)
    inverse = lax.rsqrt(variance + EPSILON)
    return centred * inverse, inverse


def head_norm_back(incoming, normed, inverse, gain):
    scaled = incoming * gain
    return (
        scaled
        - jnp.mean(scaled, axis=-1, keepdims=True)
        - normed * jnp.mean(scaled * normed, axis=-1, keepdims=True)
    ) * inverse


def kernel(
    src_ref, off_ref, qg_ref, kg_ref, patches_ref, cot_ref, wq_hbm, wo_hbm,
    block_ref, pgrad_ref, qkv_ref, out_ref,
    wq, wo, xf, gf, term, pj, gp, att, ga, qb, kb, probs, bias, sel_t, pack, own_x, own_g,
    og, ar, og2, ar2, rb1, rb2, pq, cq, rq, po, co, ro, ssem, rsem, lsem,
):
    dp, mp = lax.axis_index("dp"), lax.axis_index("mp")
    x, c = dp // 2, dp % 2
    y, z = mp // RING, mp % RING
    counter = [0]

    def at_mp(yy, zz):
        return (dp, (yy % RING) * RING + zz % RING)

    def at_dp(xx, cc):
        return ((xx % RING) * 2 + cc, mp)

    def along(axis, step):
        if axis == "y":
            return at_mp(y + RING + step, z)
        if axis == "z":
            return at_mp(y, z + RING + step)
        return at_dp(x + RING + step, c)

    def remote(src, dst, device):
        k = counter[0]
        counter[0] += 1
        return pltpu.make_async_remote_copy(
            src_ref=src, dst_ref=dst, send_sem=ssem.at[k], recv_sem=rsem.at[k],
            device_id=device, device_id_type=MESH,
        )

    sent = {}

    def start(copy):
        copy.start()
        sent[id(copy)] = copy

    def settle(copies):
        for copy in copies:
            sent.pop(id(copy)).wait_send()

    def column(dy, dz):
        block = ((y + dy) % RING) * RING + (z + dz) % RING
        return pl.ds(pl.multiple_of(block * FEAT, 128), FEAT)

    class Gather:
        def __init__(self, full):
            self.full = full
            self.one, self.fwd, self.two, self.fwd2 = {}, {}, {}, {}
            for h in (0, 1):
                a, b = ("y", "z") if h == 0 else ("z", "y")
                for s in (1, -1):
                    self.one[h, s] = self.copy(h, 0, 0, 0, HALF, a, s)
                    self.fwd[h, s] = self.copy(h, -s, 0, 0 if s == 1 else QUART, QUART, a, s)
                    for da in (0, 1, -1, 2):
                        self.two[h, da, s] = self.copy(h, da, 0, 0, HALF, b, s)
                        self.fwd2[h, da, s] = self.copy(h, da, -s, 0 if s == 1 else QUART, QUART, b, s)

        def copy(self, h, da, db, low, n, axis, s):
            dy, dz = (da, db) if h == 0 else (db, da)
            ref = self.full.at[pl.ds(h * HALF + low, n), column(dy + RING, dz + RING)]
            return remote(ref, ref, along(axis, s))

        def begin(self):
            for s in (1, -1):
                for h in (0, 1):
                    start(self.one[h, s])

        def second(self, da):
            for s in (1, -1):
                for h in (0, 1):
                    start(self.two[h, da, s])

        def forward(self, then=True):
            for s in (1, -1):
                for h in (0, 1):
                    self.one[h, s].wait_recv()
                    start(self.fwd[h, s])
            if then:
                self.second(1)
                self.second(-1)

        def opposite(self):
            for s in (1, -1):
                for h in (0, 1):
                    self.fwd[h, s].wait_recv()

        def forward2(self, da):
            for s in (1, -1):
                for h in (0, 1):
                    self.two[h, da, s].wait_recv()
                    start(self.fwd2[h, da, s])

        def copies(self):
            return [copy for group in (self.one, self.fwd, self.two, self.fwd2) for copy in group.values()]

        def finish(self, das=(0, 1, -1, 2)):
            for da in das:
                for s in (1, -1):
                    for h in (0, 1):
                        self.fwd2[h, da, s].wait_recv()

    class Ring:
        def __init__(self, part, box, rows, axis, chunk=None):
            half = rows // 2
            self.part, self.box, self.rows, self.half = part, box, rows, half
            self.chunk = chunk
            self.c0 = remote(part(2, 0, half), box(0, half), along(axis, 1))
            self.c1 = remote(part(2, half, half), box(half, half), along(axis, -1))
            self.c2 = remote(part(1, half, half), box(rows + half, half), along(axis, 1))
            self.c3 = remote(part(3, 0, half), box(2 * rows, half), along(axis, -1))
            self.c4 = remote(part(1, 0, half), box(rows, half), along(axis, 1))
            self.c5 = remote(part(3, half, half), box(2 * rows + half, half), along(axis, -1))

        def far(self):
            start(self.c0)
            start(self.c1)

        def near(self):
            start(self.c2)
            start(self.c3)

        def add(self, r, low, box_low):
            if self.chunk is None:
                ref = self.part(r, low, self.half)
                ref[...] = (ref[...].astype(F32) + self.box(box_low, self.half)[...].astype(F32)).astype(BF)
                return

            @pl.loop(0, self.half // self.chunk)
            def _(i):
                step = pl.multiple_of(i * self.chunk, self.chunk)
                ref = self.part(r, low + step, self.chunk)
                ref[...] = (ref[...].astype(F32) + self.box(box_low + step, self.chunk)[...].astype(F32)).astype(BF)

        def pass_on(self):
            self.c0.wait_recv()
            self.add(1, 0, 0)
            start(self.c4)
            self.c1.wait_recv()
            self.add(3, self.half, self.half)
            start(self.c5)

        def arrive(self):
            for copy in (self.c2, self.c3, self.c4, self.c5):
                copy.wait_recv()

        def total(self, low, n):
            return (
                self.part(0, low, n)[...].astype(F32)
                + self.box(self.rows + low, n)[...].astype(F32)
                + self.box(2 * self.rows + low, n)[...].astype(F32)
            )

    class Scatter:
        def __init__(self, terms, boxes):
            self.first, self.last = {}, {}
            for h in (0, 1):
                a, b = ("z", "y") if h == 0 else ("y", "z")

                def piece(r1, r2, low, n, h=h):
                    slot = r2 * RING + r1 if h == 0 else r1 * RING + r2
                    return terms.at[pl.ds(h * HALF + low, n), pl.ds(slot * FEAT, FEAT)]

                for r2 in range(RING):
                    self.first[h, r2] = Ring(
                        lambda r, low, n, r2=r2, piece=piece: piece(r, r2, low, n),
                        lambda low, n, h=h, r2=r2: boxes.at[h, r2, pl.ds(low, n)],
                        HALF, a,
                    )
                self.last[h] = Ring(
                    lambda r, low, n, piece=piece: piece(0, r, low, n),
                    lambda low, n, h=h: boxes.at[h, RING, pl.ds(low, n)],
                    HALF, b,
                )

        def send(self, r2):
            for h in (0, 1):
                self.first[h, r2].far()
            for h in (0, 1):
                self.first[h, r2].near()

        def pass_on(self, r2):
            for h in (0, 1):
                self.first[h, r2].pass_on()

        def collect(self, r2):
            for h in (0, 1):
                ring = self.first[h, r2]
                ring.arrive()
                ring.part(0, 0, HALF)[...] = ring.total(0, HALF).astype(BF)
                if r2 == 2:
                    self.last[h].far()
            if r2 == 3:
                for h in (0, 1):
                    self.last[h].near()

        def last_pass(self):
            for h in (0, 1):
                self.last[h].pass_on()

        def result(self, h):
            self.last[h].arrive()
            return self.last[h].total(0, HALF)

    class WeightGrad:
        def __init__(self, rows, cols, width, mine, theirs, boxes, slots, result):
            self.rows, self.cols, self.mine, self.theirs, self.result = rows, cols, mine, theirs, result
            self.slots = slots
            self.swap = {
                dx: remote(mine.at[i % slots], theirs.at[dx], at_dp(x, 1 - c)) for i, dx in enumerate((2, 1, 3, 0))
            }
            self.ring = Ring(
                lambda r, low, n: theirs.at[r, pl.ds(low, n)], lambda low, n: boxes.at[pl.ds(low, n)],
                GRAD_ROWS, "x", chunk=64,
            )
            self.order = []

        def tile(self, dx, core, m):
            block = ((x + dx) % RING) * 2 + core
            left = self.rows[:, pl.ds(pl.multiple_of(block * GRAD_ROWS + m * 256, 128), 256)]
            return dot_tn(left, self.cols[...])

        def send(self, dx):
            i = len(self.order)
            if i >= self.slots:
                self.swap[self.order[i - self.slots]].wait_send()
            self.order.append(dx)
            slot = i % self.slots

            @pl.loop(0, GRAD_ROWS // 256)
            def _(m):
                self.mine[slot, pl.ds(pl.multiple_of(m * 256, 256), 256), :] = self.tile(dx, 1 - c, m).astype(BF)

            self.swap[dx].start()

        def add(self, dx):
            self.swap[dx].wait_recv()

            @pl.loop(0, GRAD_ROWS // 256)
            def _(m):
                at = pl.ds(pl.multiple_of(m * 256, 256), 256)
                value = self.tile(dx, c, m) + self.theirs[dx, at, :].astype(F32)
                if dx == 0:
                    self.result[at, :] = value
                else:
                    self.theirs[dx, at, :] = value.astype(BF)

            if dx == 2:
                self.ring.far()
            if dx == 3:
                self.ring.near()

        def finish(self):
            self.ring.arrive()

            @pl.loop(0, GRAD_ROWS // 64)
            def _(i):
                low = pl.multiple_of(i * 64, 64)
                at = pl.ds(low, 64)
                self.result[at, :] = (
                    self.result[at, :]
                    + self.ring.box(GRAD_ROWS + low, 64)[...].astype(F32)
                    + self.ring.box(2 * GRAD_ROWS + low, 64)[...].astype(F32)
                )

        def close(self):
            for dx in self.order[-self.slots:]:
                self.swap[dx].wait_send()

    load_q = pltpu.make_async_copy(wq_hbm, wq, lsem.at[0])
    load_o = pltpu.make_async_copy(wo_hbm, wo, lsem.at[1])
    load_q.start()
    load_o.start()

    barrier = pltpu.get_barrier_semaphore()
    for axis in ("y", "z"):
        for s in (1, -1):
            pl.semaphore_signal(barrier, inc=1, device_id=along(axis, s), device_id_type=MESH)
    for o in range(1, N_DP):
        pl.semaphore_signal(barrier, inc=1, device_id=((dp + o) % N_DP, mp), device_id_type=MESH)

    off = off_ref[...]
    total_rows = jnp.sum((off >= 0).astype(F32), axis=1, keepdims=True)
    row_id = lax.broadcasted_iota(jnp.int32, (ROWS, ROWS), 0)
    col_id = lax.broadcasted_iota(jnp.int32, (ROWS, ROWS), 1)
    row_live = row_id.astype(F32) < total_rows
    col_live = col_id.astype(F32) < total_rows
    sel_t[...] = (row_id == src_ref[...]).astype(F32).astype(BF)
    pack[...] = (row_id == off).astype(F32).astype(BF)
    own_g[...] = jnp.where(row_live, cot_ref[...].astype(F32), 0.0).astype(BF)
    gf[:, column(0, 0)] = own_g[...]
    og[...] = dot_tn(sel_t[...], patches_ref[...]).astype(BF)

    gather_g, gather_x = Gather(gf), Gather(xf)
    swap_x = [
        remote(og.at[pl.ds(pl.multiple_of(((dp + o) % N_DP) * SLOTS, SLOTS), SLOTS)],
               ar.at[pl.ds(pl.multiple_of(dp * SLOTS, SLOTS), SLOTS)], ((dp + o) % N_DP, mp))
        for o in range(1, N_DP)
    ]
    swap_g = [
        remote(og2.at[pl.ds(pl.multiple_of(((dp + o) % N_DP) * SLOTS, SLOTS), SLOTS)],
               ar2.at[pl.ds(pl.multiple_of(dp * SLOTS, SLOTS), SLOTS)], ((dp + o) % N_DP, mp))
        for o in range(1, N_DP)
    ]
    scatter_p, scatter_b = Scatter(term, rb1), Scatter(gf, rb2)
    grad_q = WeightGrad(xf, gp, QKV, pq, cq, rq, 2, qkv_ref)
    grad_o = WeightGrad(gf, att, OUT, po, co, ro, 4, out_ref)
    assert counter[0] <= N_SEMS

    pl.semaphore_wait(barrier, 4 + N_DP - 1)
    for copy in swap_x:
        start(copy)
    gather_g.begin()
    here = pl.ds(pl.multiple_of(dp * SLOTS, SLOTS), SLOTS)
    ar[here, :] = og[here, :]
    same = ((row_id * 1366) >> 16) == ((col_id * 1366) >> 16)
    image = dot(pack[...], same.astype(F32).astype(BF)).astype(BF)
    both = dot_nt(image, pack[...]) > 0.5
    bias[...] = jnp.where(both | (jnp.logical_not(row_live) & jnp.logical_not(col_live)), 0.0, -jnp.inf)
    for copy in swap_x:
        copy.wait_recv()
    own_x[...] = dot(pack[...], ar[...]).astype(BF)
    xf[:, column(0, 0)] = own_x[...]
    gather_x.begin()
    gather_x.second(0)
    gather_g.forward(then=False)
    gather_x.forward()
    gather_g.opposite()
    gather_x.opposite()
    gather_x.second(2)
    for da in (0, 1, -1):
        gather_x.forward2(da)
    for da in (0, 1, -1, 2):
        gather_g.second(da)
    gather_x.forward2(2)
    gather_x.finish()
    load_q.wait()
    load_o.wait()

    def project(low, high):
        @pl.loop(low, high)
        def _(k):
            at = pl.ds(pl.multiple_of(k * 768, 768), 768)
            part = dot(xf[:, at], wq[at, :])

            @pl.when(k == 0)
            def _():
                qkv_ref[0:ROWS, :] = part

            @pl.when(k > 0)
            def _():
                qkv_ref[0:ROWS, :] += part

    def head_forward(h):
        base = h * 3 * HEAD
        query, _ = head_norm(pj[:, base:base + HEAD].astype(F32))
        keys, _ = head_norm(pj[:, base + HEAD:base + 2 * HEAD].astype(F32))
        qb[h] = (query * qg_ref[...]).astype(BF)
        kb[h] = (keys * kg_ref[...]).astype(BF)
        scores = dot_nt(qb[h], kb[h]) * SCALE + bias[...]
        exponent = jnp.exp(scores - jnp.max(scores, axis=-1, keepdims=True))
        prob = exponent / jnp.sum(exponent, axis=-1, keepdims=True)
        probs[h] = prob
        att[:, h * HEAD:(h + 1) * HEAD] = dot(prob.astype(BF), pj[:, base + 2 * HEAD:base + 3 * HEAD]).astype(BF)

    def head_backward(h):
        base = h * 3 * HEAD
        value = pj[:, base + 2 * HEAD:base + 3 * HEAD]
        incoming = ga[:, h * HEAD:(h + 1) * HEAD]
        prob = probs[h]
        gp[:, base + 2 * HEAD:base + 3 * HEAD] = dot_tn(prob.astype(BF), incoming).astype(BF)
        grad_probs = dot_nt(incoming, value)
        grad_scores = (prob * (grad_probs - jnp.sum(prob * grad_probs, axis=-1, keepdims=True)) * SCALE).astype(BF)
        query, query_inv = head_norm(pj[:, base:base + HEAD].astype(F32))
        keys, key_inv = head_norm(pj[:, base + HEAD:base + 2 * HEAD].astype(F32))
        grad_qn = dot(grad_scores, kb[h])
        grad_kn = dot_tn(grad_scores, qb[h])
        gp[:, base:base + HEAD] = head_norm_back(grad_qn, query, query_inv, qg_ref[...]).astype(BF)
        gp[:, base + HEAD:base + 2 * HEAD] = head_norm_back(grad_kn, keys, key_inv, kg_ref[...]).astype(BF)

    def make_terms(low, high, left, weights, terms):
        @pl.loop(low, high)
        def _(j):
            block = ((y + j // RING) % RING) * RING + (z + j % RING) % RING
            at = pl.ds(pl.multiple_of(block * FEAT, 128), FEAT)
            value = dot_nt(left[...], weights[at, :]).astype(BF)
            terms[:, pl.ds(pl.multiple_of(j * FEAT, 128), FEAT)] = value

    project(0, 3)
    gather_g.forward2(0)
    project(3, 6)
    gather_g.forward2(1)
    project(6, 8)
    pj[...] = qkv_ref[0:ROWS, :].astype(BF)
    gather_g.forward2(-1)
    head_forward(0)
    gather_g.forward2(2)
    head_forward(1)
    make_terms(0, 16, att, wo, term)
    for r2 in (2, 1, 3, 0):
        scatter_p.send(r2)
    gather_g.finish()

    def grad_attended():
        @pl.loop(0, 8)
        def _(k):
            at = pl.ds(pl.multiple_of(k * 768, 768), 768)
            part = dot(gf[:, at], wo[at, :])

            @pl.when(k == 0)
            def _():
                qkv_ref[0:ROWS, 0:OUT] = part

            @pl.when(k > 0)
            def _():
                qkv_ref[0:ROWS, 0:OUT] += part

        ga[...] = qkv_ref[0:ROWS, 0:OUT].astype(BF)

    grad_o.send(2)
    grad_o.send(1)
    grad_o.add(2)
    grad_attended()
    scatter_p.pass_on(2)
    head_backward(0)
    scatter_p.pass_on(1)
    head_backward(1)
    scatter_p.pass_on(3)
    grad_q.send(2)
    grad_o.send(3)
    grad_o.send(0)
    grad_o.add(1)
    grad_o.add(3)
    grad_q.add(2)
    scatter_p.pass_on(0)
    scatter_p.collect(2)
    grad_q.send(1)
    grad_q.add(1)
    grad_o.add(0)
    scatter_p.collect(1)
    scatter_p.collect(3)
    grad_q.send(3)
    grad_q.add(3)
    grad_o.ring.pass_on()
    settle(gather_g.copies())
    make_terms(0, 16, gp, wq, gf)
    scatter_p.last_pass()
    for r2 in (2, 1, 3, 0):
        scatter_b.send(r2)
    scatter_p.collect(0)
    grad_q.send(0)
    grad_q.add(0)
    for h in (0, 1):
        rows = pl.ds(h * HALF, HALF)
        live = lax.broadcasted_iota(jnp.int32, (HALF, FEAT), 0).astype(F32) + float(h * HALF) < total_rows
        value = own_x[rows, :].astype(F32) + scatter_p.result(h)
        block_ref[rows, :] = jnp.where(live, value, 0.0).astype(BF)
    scatter_b.pass_on(2)
    scatter_b.pass_on(1)
    scatter_b.pass_on(3)
    scatter_b.pass_on(0)
    grad_o.finish()
    scatter_b.collect(2)
    grad_q.ring.pass_on()
    scatter_b.collect(1)
    scatter_b.collect(3)
    scatter_b.last_pass()
    scatter_b.collect(0)
    for h in (0, 1):
        rows = pl.ds(h * HALF, HALF)
        own_g[rows, :] = (own_g[rows, :].astype(F32) + scatter_b.result(h)).astype(BF)
    og2[...] = dot_tn(pack[...], own_g[...]).astype(BF)
    for copy in swap_g:
        start(copy)
    ar2[here, :] = og2[here, :]
    grad_q.finish()
    for copy in swap_g:
        copy.wait_recv()
    pgrad_ref[...] = dot(sel_t[...], ar2[...]).astype(BF)
    grad_q.close()
    grad_o.close()
    settle(list(sent.values()))


def shards(
    patches, keep_index, keep_count, pack_dest, pack_offset, w_qkv, q_gain, k_gain, w_out, cotangent
):
    shard = lax.axis_index("dp")
    places = jnp.arange(N_DP, dtype=jnp.int32)
    lanes = jnp.arange(SLOTS, dtype=jnp.int32)
    dest = pack_dest.reshape(N_DP, N_DP)
    count = keep_count.reshape(N_DP, N_DP)
    offset = pack_offset.reshape(N_DP, N_DP)
    my_dest = lax.dynamic_index_in_dim(dest, shard, 0, keepdims=False)
    my_count = lax.dynamic_index_in_dim(count, shard, 0, keepdims=False)
    rows = keep_index + places[:, None] * SLOTS + 1
    rows = jnp.where(lanes[None, :] < my_count[:, None], rows, 0)
    source = jnp.sum(jnp.where(my_dest[None, :, None] == places[:, None, None], rows[None], 0), axis=1) - 1
    mine = dest == shard
    got = jnp.sum(jnp.where(mine, count, 0), axis=1)
    base = jnp.sum(jnp.where(mine, offset, 0), axis=1)
    target = jnp.where(lanes[None, :] < got[:, None], base[:, None] + lanes[None, :], -1)

    vmem = pl.BlockSpec(memory_space=pltpu.VMEM)
    hbm = pl.BlockSpec(memory_space=pltpu.HBM)
    return pl.pallas_call(
        kernel,
        out_shape=(
            jax.ShapeDtypeStruct((ROWS, FEAT), BF),
            jax.ShapeDtypeStruct((ROWS, FEAT), BF),
            jax.ShapeDtypeStruct((GRAD_ROWS, QKV), F32),
            jax.ShapeDtypeStruct((GRAD_ROWS, OUT), F32),
        ),
        in_specs=[vmem] * 6 + [hbm] * 2,
        out_specs=(vmem,) * 4,
        scratch_shapes=[
            pltpu.VMEM((D, QKV), BF),
            pltpu.VMEM((D, OUT), BF),
            pltpu.VMEM((ROWS, D), BF),
            pltpu.VMEM((ROWS, D), BF),
            pltpu.VMEM((ROWS, D), BF),
            pltpu.VMEM((ROWS, QKV), BF),
            pltpu.VMEM((ROWS, QKV), BF),
            pltpu.VMEM((ROWS, OUT), BF),
            pltpu.VMEM((ROWS, OUT), BF),
            pltpu.VMEM((HEADS_DEV, ROWS, HEAD), BF),
            pltpu.VMEM((HEADS_DEV, ROWS, HEAD), BF),
            pltpu.VMEM((HEADS_DEV, ROWS, ROWS), F32),
            pltpu.VMEM((ROWS, ROWS), F32),
            pltpu.VMEM((ROWS, ROWS), BF),
            pltpu.VMEM((ROWS, ROWS), BF),
            pltpu.VMEM((ROWS, FEAT), BF),
            pltpu.VMEM((ROWS, FEAT), BF),
            pltpu.VMEM((ROWS, FEAT), BF),
            pltpu.VMEM((ROWS, FEAT), BF),
            pltpu.VMEM((ROWS, FEAT), BF),
            pltpu.VMEM((ROWS, FEAT), BF),
            pltpu.VMEM((2, RING + 1, 3 * HALF, FEAT), BF),
            pltpu.VMEM((2, RING + 1, 3 * HALF, FEAT), BF),
            pltpu.VMEM((2, GRAD_ROWS, QKV), BF),
            pltpu.VMEM((RING, GRAD_ROWS, QKV), BF),
            pltpu.VMEM((3 * GRAD_ROWS, QKV), BF),
            pltpu.VMEM((4, GRAD_ROWS, OUT), BF),
            pltpu.VMEM((RING, GRAD_ROWS, OUT), BF),
            pltpu.VMEM((3 * GRAD_ROWS, OUT), BF),
            pltpu.SemaphoreType.DMA((N_SEMS,)),
            pltpu.SemaphoreType.DMA((N_SEMS,)),
            pltpu.SemaphoreType.DMA((2,)),
        ],
        compiler_params=pltpu.CompilerParams(
            collective_id=0, has_side_effects=True, vmem_limit_bytes=63 << 20
        ),
        cost_estimate=pl.CostEstimate(flops=15_000_000_000, bytes_accessed=20_000_000, transcendentals=300_000),
        name="block",
    )(
        source.reshape(1, ROWS), target.reshape(1, ROWS), q_gain.reshape(1, HEAD), k_gain.reshape(1, HEAD),
        patches, cotangent, w_qkv, w_out,
    )


def solution(mesh):
    placed = (
        P("dp", "mp"), P("dp", None), P(), P(), P(), P(None, "mp"), P(), P(), P(None, "mp"), P("dp", "mp"),
    )
    return jax.shard_map(
        shards, mesh=mesh, in_specs=placed, out_specs=(P("dp", "mp"),) * 4, check_vma=False,
    )
```

time: 474 us -> 162 us (0.34)
  waiting for transfers between devices: 308 us -> 0 us
  Pallas kernels: 0 us -> 149 us
  matrix products: 64.1 us -> 0 us
  other arithmetic: 34.4 us -> 1.08 us
  local copies, waits for them, and re-layouts: 38.3 us -> 11.1 us
  between operations: 14.4 us -> 0.69 us
  starting transfers between devices: 13.1 us -> 0 us
    pallas_call x0 -> x1, Pallas kernels: none -> 149 us  [shards(): pl.pallas_call(kernel, out_shape=(jax.ShapeDtypeStruct((ROWS, FEAT), BF),...]
    unnamed x8 -> x0, waiting for transfers between devices: 129 us -> none
    all_gather x2 -> x0, waiting for transfers between devices: 103 us -> none  [widen(): return lax.all_gather(local_rows, 'mp', axis=1, tiled=True)]
    reduce_scatter x2 -> x0, waiting for transfers between devices: 75.6 us -> none  [the longest x1 51.8 us: shards(): lax.psum_scatter(qkv_part.astype(jnp.bfloat16), 'dp', scatter_dimension=0...]
    dot_general x11 -> x0, matrix products: 61.4 us -> none  [the longest x2 18.2 us: contract_columns(): lax.dot_general(left, right, (((1,), (1,)), ((), ())), preferred_element_...]
    gather x10 -> x0, local copies, waits for them, and re-layouts: 14.7 us -> none  [the longest x1 2.54 us: shards(): jnp.take(grad_packed, back_rows.reshape(-1), axis=0)]
    all_to_all x2 -> x0, starting transfers between devices: 12.5 us -> none  [the longest x1 6.67 us: shards(): lax.all_to_all(outgoing_grad, 'dp', split_axis=0, concat_axis=0, tiled=True)]
    unnamed x38 -> x6, local copies, waits for them, and re-layouts: 19.5 us -> 7.59 us
  transfers between devices with their start and end apart: 8 -> 0, of which waited for: 6 -> 0; matrix products, arithmetic and copies ran while one was open for 15% -> 0% of each run, Pallas kernels for 0% -> 0%
where the time goes in v1:
time: 162 us
  Pallas kernels  149 us (92%)
  local copies, waits for them, and re-layouts  11.1 us (7%)
    pallas_call x1, Pallas kernels, shards(): pl.pallas_call(kernel, out_shape=(jax.ShapeDtypeStruct((ROWS, FEAT), BF),...  149 us
    unnamed x6, local copies, waits for them, and re-layouts  7.59 us

profile of v1, /device:TPU:1, one launch (start us, length us, event | category | flops | bytes accessed | tf_op | source)
XLA Modules:
  0.0 161.7 jit_solution(15998475898667708757)
XLA Ops:
  0.6 0.7 reshape.123
  1.4 0.7 reshape.122
  2.1 0.8 add_select_fusion.1
  2.9 0.1 select_reduce_fusion
  3.0 0.6 sub.6.src_ref
  3.6 0.7 reshape.124
  4.4 0.1 select_reduce_fusion.2
  4.5 0.1 add_select_fusion
  4.6 0.7 select_n.39.off_ref
  5.3 148.8 %block.1 = (bf16[384,384]{1,0:T(8,128)(2,1)}, bf16[384,384]{1,0:T(8,128)(2,1)}, f32[768,768]{1,0:T(8,128)}, f32[768,256]{1,0:T(8,128)}) custom-call(s32[1,384]{1,0:T(1,128)} %sub.6.src_ref, s32[1,384]{1,0:T(1,128)} %select_n.39.off_ref, f32[1,128]{1,0:T(1,128)} %bitcast.6, f32[1,128]{1,0:T(1,128)} %bitcast.7, bf16[384,384]{1,0:T(8,128)(2,1)} %patches_ref.1, ...), custom_call_target="tpu_custom_call" | custom-call | flops 15000000512 | bytes 20000000 | tf_op jit(solution)/shard_map/block/pallas_call | solution.py:562
  154.1 0.0 copy-start
  154.1 1.8 %copy.18 = bf16[384,384]{1,0:T(8,128)(2,1)} copy(bf16[384,384]{1,0:T(8,128)(2,1)} %get-tuple-element.12) | data formatting | bytes 589824
  155.9 1.7 %copy.19 = bf16[384,384]{1,0:T(8,128)(2,1)} copy(bf16[384,384]{1,0:T(8,128)(2,1)} %get-tuple-element.13) | data formatting | bytes 589824
  157.6 3.2 %copy.20 = f32[768,768]{1,0:T(8,128)} copy(f32[768,768]{1,0:T(8,128)} %get-tuple-element.14) | data formatting | bytes 4718592
  160.8 0.0 copy-done
  160.8 0.9 copy.21
  (4 shorter events, 0.0 us)
Async XLA Ops:
  154.1 6.7 %copy-start = (f32[768,256]{1,0:T(8,128)S(1)}, f32[768,256]{1,0:T(8,128)}, u32[]{:S(2)}) copy-start(f32[768,256]{1,0:T(8,128)} %get-tuple-element.15) | copy-start | bytes 2359300

commit v2 on v1

--- a/solution.py
+++ b/solution.py
@@ -54,7 +54,8 @@
 
 
 def kernel(
-    src_ref, off_ref, qg_ref, kg_ref, patches_ref, cot_ref, wq_hbm, wo_hbm,
+    count_ref, dest_ref, offset_ref, keep_ref, qg_ref, kg_ref, patches_ref, cot_ref, wq_hbm, wo_hbm,
+    block_hbm, pgrad_hbm, qkv_hbm, out_hbm,
     block_ref, pgrad_ref, qkv_ref, out_ref,
     wq, wo, xf, gf, term, pj, gp, att, ga, qb, kb, probs, bias, sel_t, pack, own_x, own_g,
     og, ar, og2, ar2, rb1, rb2, pq, cq, rq, po, co, ro, ssem, rsem, lsem,
@@ -335,16 +336,38 @@
     for o in range(1, N_DP):
         pl.semaphore_signal(barrier, inc=1, device_id=((dp + o) % N_DP, mp), device_id_type=MESH)
 
-    off = off_ref[...]
-    total_rows = jnp.sum((off >= 0).astype(F32), axis=1, keepdims=True)
+    def saved(copy):
+        copy.start()
+        saves.append(copy)
+
+    saves = []
+    lane = lax.broadcasted_iota(jnp.int32, (1, ROWS), 1)
+    part = (lane * 1366) >> 16
+    slot = lane - part * SLOTS
+    off = jnp.full((1, ROWS), -1, jnp.int32)
+    total_rows = 0
+    for t in range(N_DP):
+        base, here_count = 0, 0
+        for k in range(N_DP):
+            mine = dest_ref[t * N_DP + k] == dp
+            base += jnp.where(mine, offset_ref[t * N_DP + k], 0)
+            here_count += jnp.where(mine, count_ref[t * N_DP + k], 0)
+        off = jnp.where((part == t) & (slot < here_count), base + slot, off)
+        total_rows += here_count
+    spread_row = lax.broadcasted_iota(jnp.int32, (SLOTS, ROWS), 0)
+    spread = (spread_row == slot).astype(F32).astype(BF)
+    kept = dot(keep_ref[...].astype(F32).astype(BF), spread).astype(jnp.int32)
+    src = jnp.full((1, ROWS), -1, jnp.int32)
+    for k in range(N_DP):
+        goes = (part == dest_ref[dp * N_DP + k]) & (slot < count_ref[dp * N_DP + k])
+        src = jnp.where(goes, kept[k:k + 1, :] + k * SLOTS, src)
     row_id = lax.broadcasted_iota(jnp.int32, (ROWS, ROWS), 0)
     col_id = lax.broadcasted_iota(jnp.int32, (ROWS, ROWS), 1)
-    row_live = row_id.astype(F32) < total_rows
-    col_live = col_id.astype(F32) < total_rows
-    sel_t[...] = (row_id == src_ref[...]).astype(F32).astype(BF)
-    pack[...] = (row_id == off).astype(F32).astype(BF)
+    row_live = row_id < total_rows
+    col_live = col_id < total_rows
     own_g[...] = jnp.where(row_live, cot_ref[...].astype(F32), 0.0).astype(BF)
     gf[:, column(0, 0)] = own_g[...]
+    sel_t[...] = (row_id == src).astype(F32).astype(BF)
     og[...] = dot_tn(sel_t[...], patches_ref[...]).astype(BF)
 
     gather_g, gather_x = Gather(gf), Gather(xf)
@@ -369,10 +392,7 @@
     gather_g.begin()
     here = pl.ds(pl.multiple_of(dp * SLOTS, SLOTS), SLOTS)
     ar[here, :] = og[here, :]
-    same = ((row_id * 1366) >> 16) == ((col_id * 1366) >> 16)
-    image = dot(pack[...], same.astype(F32).astype(BF)).astype(BF)
-    both = dot_nt(image, pack[...]) > 0.5
-    bias[...] = jnp.where(both | (jnp.logical_not(row_live) & jnp.logical_not(col_live)), 0.0, -jnp.inf)
+    pack[...] = (row_id == off).astype(F32).astype(BF)
     for copy in swap_x:
         copy.wait_recv()
     own_x[...] = dot(pack[...], ar[...]).astype(BF)
@@ -384,14 +404,18 @@
     gather_g.opposite()
     gather_x.opposite()
     gather_x.second(2)
+    same = ((row_id * 1366) >> 16) == ((col_id * 1366) >> 16)
+    image = dot(pack[...], same.astype(F32).astype(BF)).astype(BF)
+    both = dot_nt(image, pack[...]) > 0.5
+    bias[...] = jnp.where(both | (jnp.logical_not(row_live) & jnp.logical_not(col_live)), 0.0, -jnp.inf)
     for da in (0, 1, -1):
         gather_x.forward2(da)
-    for da in (0, 1, -1, 2):
+    gather_g.second(0)
+    gather_x.forward2(2)
+    for da in (1, -1, 2):
         gather_g.second(da)
-    gather_x.forward2(2)
     gather_x.finish()
     load_q.wait()
-    load_o.wait()
 
     def project(low, high):
         @pl.loop(low, high)
@@ -434,27 +458,40 @@
         gp[:, base:base + HEAD] = head_norm_back(grad_qn, query, query_inv, qg_ref[...]).astype(BF)
         gp[:, base + HEAD:base + 2 * HEAD] = head_norm_back(grad_kn, keys, key_inv, kg_ref[...]).astype(BF)
 
-    def make_terms(low, high, left, weights, terms):
-        @pl.loop(low, high)
-        def _(j):
-            block = ((y + j // RING) % RING) * RING + (z + j % RING) % RING
+    def make_terms(group, left, weights, terms):
+        @pl.loop(0, (5, 4, 7)[group])
+        def _(i):
+            if group == 0:
+                late = i // 3
+                dy = (1 - late) * 2 + late * (2 * i - 5)
+                dz = (1 - late) * (i + 1) + late * 2
+            elif group == 1:
+                dy, dz = 1 + 2 * (i // 2), 1 + 2 * (i % 2)
+            else:
+                late = i // 4
+                dy, dz = late * (i - 3), (1 - late) * i
+            block = ((y + dy) % RING) * RING + (z + dz) % RING
             at = pl.ds(pl.multiple_of(block * FEAT, 128), FEAT)
             value = dot_nt(left[...], weights[at, :]).astype(BF)
-            terms[:, pl.ds(pl.multiple_of(j * FEAT, 128), FEAT)] = value
-
-    project(0, 3)
+            terms[:, pl.ds(pl.multiple_of((dy * RING + dz) * FEAT, 128), FEAT)] = value
+
+    project(0, 4)
     gather_g.forward2(0)
-    project(3, 6)
+    project(4, 8)
     gather_g.forward2(1)
-    project(6, 8)
     pj[...] = qkv_ref[0:ROWS, :].astype(BF)
+    head_forward(0)
     gather_g.forward2(-1)
-    head_forward(0)
+    head_forward(1)
+    load_o.wait()
+    make_terms(0, att, wo, term)
     gather_g.forward2(2)
-    head_forward(1)
-    make_terms(0, 16, att, wo, term)
-    for r2 in (2, 1, 3, 0):
-        scatter_p.send(r2)
+    scatter_p.send(2)
+    make_terms(1, att, wo, term)
+    scatter_p.send(1)
+    scatter_p.send(3)
+    make_terms(2, att, wo, term)
+    scatter_p.send(0)
     gather_g.finish()
 
     def grad_attended():
@@ -476,50 +513,56 @@
     grad_o.send(2)
     grad_o.send(1)
     grad_o.add(2)
+    scatter_p.pass_on(2)
     grad_attended()
-    scatter_p.pass_on(2)
-    head_backward(0)
-    scatter_p.pass_on(1)
-    head_backward(1)
-    scatter_p.pass_on(3)
-    grad_q.send(2)
     grad_o.send(3)
-    grad_o.send(0)
     grad_o.add(1)
     grad_o.add(3)
+    scatter_p.pass_on(1)
+    head_backward(0)
+    scatter_p.pass_on(3)
+    head_backward(1)
+    grad_q.send(2)
+    scatter_p.pass_on(0)
+    grad_o.send(0)
+    grad_q.send(1)
     grad_q.add(2)
-    scatter_p.pass_on(0)
+    grad_o.add(0)
+    grad_o.ring.pass_on()
     scatter_p.collect(2)
-    grad_q.send(1)
-    grad_q.add(1)
-    grad_o.add(0)
+    settle(gather_g.copies())
+    make_terms(0, gp, wq, gf)
+    scatter_b.send(2)
     scatter_p.collect(1)
     scatter_p.collect(3)
+    make_terms(1, gp, wq, gf)
+    scatter_b.send(1)
+    scatter_b.send(3)
+    scatter_p.last_pass()
+    make_terms(2, gp, wq, gf)
+    scatter_b.send(0)
+    scatter_p.collect(0)
+    grad_q.add(1)
     grad_q.send(3)
-    grad_q.add(3)
-    grad_o.ring.pass_on()
-    settle(gather_g.copies())
-    make_terms(0, 16, gp, wq, gf)
-    scatter_p.last_pass()
-    for r2 in (2, 1, 3, 0):
-        scatter_b.send(r2)
-    scatter_p.collect(0)
-    grad_q.send(0)
-    grad_q.add(0)
+    scatter_b.pass_on(2)
     for h in (0, 1):
         rows = pl.ds(h * HALF, HALF)
-        live = lax.broadcasted_iota(jnp.int32, (HALF, FEAT), 0).astype(F32) + float(h * HALF) < total_rows
+        live = lax.broadcasted_iota(jnp.int32, (HALF, FEAT), 0) + h * HALF < total_rows
         value = own_x[rows, :].astype(F32) + scatter_p.result(h)
         block_ref[rows, :] = jnp.where(live, value, 0.0).astype(BF)
-    scatter_b.pass_on(2)
+    saved(pltpu.make_async_copy(block_ref, block_hbm, lsem.at[2]))
     scatter_b.pass_on(1)
     scatter_b.pass_on(3)
+    grad_q.add(3)
     scatter_b.pass_on(0)
-    grad_o.finish()
+    grad_q.send(0)
+    grad_q.ring.pass_on()
     scatter_b.collect(2)
-    grad_q.ring.pass_on()
+    grad_q.add(0)
     scatter_b.collect(1)
     scatter_b.collect(3)
+    grad_o.finish()
+    saved(pltpu.make_async_copy(out_ref, out_hbm, lsem.at[3]))
     scatter_b.last_pass()
     scatter_b.collect(0)
     for h in (0, 1):
@@ -530,46 +573,59 @@
         start(copy)
     ar2[here, :] = og2[here, :]
     grad_q.finish()
+    saved(pltpu.make_async_copy(qkv_ref, qkv_hbm, lsem.at[4]))
     for copy in swap_g:
         copy.wait_recv()
     pgrad_ref[...] = dot(sel_t[...], ar2[...]).astype(BF)
+    saved(pltpu.make_async_copy(pgrad_ref, pgrad_hbm, lsem.at[5]))
     grad_q.close()
     grad_o.close()
     settle(list(sent.values()))
+    for copy in saves:
+        copy.wait()
+
+
+def hand_over(*refs):
+    inputs, outputs, held, sems = refs[:4], refs[4:8], refs[8:12], refs[12]
+    pairs = []
+    for source, target, stage in zip(inputs, outputs, held):
+        pieces = max(1, source.shape[0] * source.shape[1] // (192 * 768))
+        step = source.shape[0] // pieces
+        for p in range(pieces):
+            at = pl.ds(p * step, step)
+            k = len(pairs)
+            pairs.append((
+                pltpu.make_async_copy(source.at[at], stage.at[at], sems.at[0, k]),
+                pltpu.make_async_copy(stage.at[at], target.at[at], sems.at[1, k]),
+            ))
+    for fetch, _ in pairs:
+        fetch.start()
+    for fetch, store in pairs:
+        fetch.wait()
+        store.start()
+    for _, store in pairs:
+        store.wait()
 
 
 def shards(
     patches, keep_index, keep_count, pack_dest, pack_offset, w_qkv, q_gain, k_gain, w_out, cotangent
 ):
-    shard = lax.axis_index("dp")
-    places = jnp.arange(N_DP, dtype=jnp.int32)
-    lanes = jnp.arange(SLOTS, dtype=jnp.int32)
-    dest = pack_dest.reshape(N_DP, N_DP)
-    count = keep_count.reshape(N_DP, N_DP)
-    offset = pack_offset.reshape(N_DP, N_DP)
-    my_dest = lax.dynamic_index_in_dim(dest, shard, 0, keepdims=False)
-    my_count = lax.dynamic_index_in_dim(count, shard, 0, keepdims=False)
-    rows = keep_index + places[:, None] * SLOTS + 1
-    rows = jnp.where(lanes[None, :] < my_count[:, None], rows, 0)
-    source = jnp.sum(jnp.where(my_dest[None, :, None] == places[:, None, None], rows[None], 0), axis=1) - 1
-    mine = dest == shard
-    got = jnp.sum(jnp.where(mine, count, 0), axis=1)
-    base = jnp.sum(jnp.where(mine, offset, 0), axis=1)
-    target = jnp.where(lanes[None, :] < got[:, None], base[:, None] + lanes[None, :], -1)
-
     vmem = pl.BlockSpec(memory_space=pltpu.VMEM)
     hbm = pl.BlockSpec(memory_space=pltpu.HBM)
-    return pl.pallas_call(
+    smem = pl.BlockSpec(memory_space=pltpu.SMEM)
+    results = (
+        jax.ShapeDtypeStruct((ROWS, FEAT), BF),
+        jax.ShapeDtypeStruct((ROWS, FEAT), BF),
+        jax.ShapeDtypeStruct((GRAD_ROWS, QKV), F32),
+        jax.ShapeDtypeStruct((GRAD_ROWS, OUT), F32),
+    )
+    done = pl.pallas_call(
         kernel,
-        out_shape=(
-            jax.ShapeDtypeStruct((ROWS, FEAT), BF),
-            jax.ShapeDtypeStruct((ROWS, FEAT), BF),
-            jax.ShapeDtypeStruct((GRAD_ROWS, QKV), F32),
-            jax.ShapeDtypeStruct((GRAD_ROWS, OUT), F32),
-        ),
-        in_specs=[vmem] * 6 + [hbm] * 2,
-        out_specs=(vmem,) * 4,
+        out_shape=results,
+        in_specs=[smem] * 3 + [vmem] * 5 + [hbm] * 2,
+        out_specs=(hbm,) * 4,
         scratch_shapes=[
+            *(pltpu.VMEM(r.shape, r.dtype) for r in results),
             pltpu.VMEM((D, QKV), BF),
             pltpu.VMEM((D, OUT), BF),
             pltpu.VMEM((ROWS, D), BF),
@@ -601,7 +657,7 @@
             pltpu.VMEM((3 * GRAD_ROWS, OUT), BF),
             pltpu.SemaphoreType.DMA((N_SEMS,)),
             pltpu.SemaphoreType.DMA((N_SEMS,)),
-            pltpu.SemaphoreType.DMA((2,)),
+            pltpu.SemaphoreType.DMA((6,)),
         ],
         compiler_params=pltpu.CompilerParams(
             collective_id=0, has_side_effects=True, vmem_limit_bytes=63 << 20
@@ -609,9 +665,20 @@
         cost_estimate=pl.CostEstimate(flops=15_000_000_000, bytes_accessed=20_000_000, transcendentals=300_000),
         name="block",
     )(
-        source.reshape(1, ROWS), target.reshape(1, ROWS), q_gain.reshape(1, HEAD), k_gain.reshape(1, HEAD),
+        keep_count, pack_dest, pack_offset, keep_index, q_gain.reshape(1, HEAD), k_gain.reshape(1, HEAD),
         patches, cotangent, w_qkv, w_out,
     )
+    return pl.pallas_call(
+        hand_over,
+        out_shape=results,
+        in_specs=[hbm] * 4,
+        out_specs=(hbm,) * 4,
+        scratch_shapes=[
+            *(pltpu.VMEM(r.shape, r.dtype) for r in results),
+            pltpu.SemaphoreType.DMA((2, 8)),
+        ],
+        name="hand_over",
+    )(*done)
 
 
 def solution(mesh):

time: 162 us -> 140 us (0.86)
  local copies, waits for them, and re-layouts: 11.1 us -> 0 us
  Pallas kernels: 149 us -> 139 us
    pallas_call x1 -> x2, Pallas kernels: 149 us -> 139 us  [the longest x1 136 us: shards(): pl.pallas_call(kernel, out_shape=results, in_specs=[smem] * 3 + [vmem] *...]
    unnamed x6 -> x0, local copies, waits for them, and re-layouts: 7.59 us -> none
    reshape x3 -> x0, local copies, waits for them, and re-layouts: 2.2 us -> none  [the longest x1 0.74 us: shards(): dest = pack_dest.reshape(N_DP, N_DP)]
where the time goes in v2:
time: 140 us
  Pallas kernels  139 us (99%)
    pallas_call x1, Pallas kernels, shards(): pl.pallas_call(kernel, out_shape=results, in_specs=[smem] * 3 + [vmem] *...  136 us
    pallas_call x1, Pallas kernels, shards(): pl.pallas_call(hand_over, out_shape=results, in_specs=[hbm] * 4, out_spec...  3.43 us

profile of v2, /device:TPU:1, one launch (start us, length us, event | category | flops | bytes accessed | tf_op | source)
XLA Modules:
  0.0 140.2 jit_solution(12851847402118701966)
XLA Ops:
  0.6 136.0 %block.1 = (bf16[384,384]{1,0:T(8,128)(2,1)}, bf16[384,384]{1,0:T(8,128)(2,1)}, f32[768,768]{1,0:T(8,128)}, f32[768,256]{1,0:T(8,128)}) custom-call(s32[64]{0:T(128)} %count_ref.1, s32[64]{0:T(128)} %dest_ref.1, s32[64]{0:T(128)} %offset_ref.1, s32[8,48]{1,0:T(8,128)} %keep_ref.1, f32[1,128]{1,0:T(1,128)} %bitcast.2, f32[1,128]{1,0:T(1,128)} %bitcast.3, ...), custom_call_target="tpu_custom_call" | custom-call | flops 15000000512 | bytes 20000000 | tf_op jit(solution)/shard_map/block/pallas_call | solution.py:622
  136.6 3.4 %hand_over.1 = (bf16[384,384]{1,0:T(8,128)(2,1)}, bf16[384,384]{1,0:T(8,128)(2,1)}, f32[768,768]{1,0:T(8,128)}, f32[768,256]{1,0:T(8,128)}) custom-call(bf16[384,384]{1,0:T(8,128)(2,1)} %get-tuple-element.8.refs_0_, bf16[384,384]{1,0:T(8,128)(2,1)} %get-tuple-element.9.refs_1_, f32[768,768]{1,0:T(8,128)} %get-tuple-element.10.refs_2_, ...), custom_call_target="tpu_custom_call" | custom-call | tf_op jit(solution)/shard_map/hand_over/pallas_call | solution.py:671

commit v3 on v2

--- a/solution.py
+++ b/solution.py
@@ -54,8 +54,9 @@
 
 
 def kernel(
-    count_ref, dest_ref, offset_ref, keep_ref, qg_ref, kg_ref, patches_ref, cot_ref, wq_hbm, wo_hbm,
+    count_hbm, dest_hbm, offset_hbm, keep_hbm, qg_hbm, kg_hbm, patches_hbm, cot_hbm, wq_hbm, wo_hbm,
     block_hbm, pgrad_hbm, qkv_hbm, out_hbm,
+    count_ref, dest_ref, offset_ref, keep_ref, qg_ref, kg_ref, patches_ref, cot_ref,
     block_ref, pgrad_ref, qkv_ref, out_ref,
     wq, wo, xf, gf, term, pj, gp, att, ga, qb, kb, probs, bias, sel_t, pack, own_x, own_g,
     og, ar, og2, ar2, rb1, rb2, pq, cq, rq, po, co, ro, ssem, rsem, lsem,
@@ -324,10 +325,17 @@
             for dx in self.order[-self.slots:]:
                 self.swap[dx].wait_send()
 
+    loads = [
+        pltpu.make_async_copy(source, target, lsem.at[6 + i])
+        for i, (source, target) in enumerate((
+            (count_hbm, count_ref), (dest_hbm, dest_ref), (offset_hbm, offset_ref), (keep_hbm, keep_ref),
+            (cot_hbm, cot_ref), (patches_hbm, patches_ref), (qg_hbm, qg_ref), (kg_hbm, kg_ref),
+        ))
+    ]
+    for copy in loads:
+        copy.start()
     load_q = pltpu.make_async_copy(wq_hbm, wq, lsem.at[0])
     load_o = pltpu.make_async_copy(wo_hbm, wo, lsem.at[1])
-    load_q.start()
-    load_o.start()
 
     barrier = pltpu.get_barrier_semaphore()
     for axis in ("y", "z"):
@@ -336,11 +344,16 @@
     for o in range(1, N_DP):
         pl.semaphore_signal(barrier, inc=1, device_id=((dp + o) % N_DP, mp), device_id_type=MESH)
 
+    load_q.start()
+    load_o.start()
+
     def saved(copy):
         copy.start()
         saves.append(copy)
 
     saves = []
+    for copy in loads:
+        copy.wait()
     lane = lax.broadcasted_iota(jnp.int32, (1, ROWS), 1)
     part = (lane * 1366) >> 16
     slot = lane - part * SLOTS
@@ -390,6 +403,7 @@
     for copy in swap_x:
         start(copy)
     gather_g.begin()
+    gather_g.second(0)
     here = pl.ds(pl.multiple_of(dp * SLOTS, SLOTS), SLOTS)
     ar[here, :] = og[here, :]
     pack[...] = (row_id == off).astype(F32).astype(BF)
@@ -410,7 +424,7 @@
     bias[...] = jnp.where(both | (jnp.logical_not(row_live) & jnp.logical_not(col_live)), 0.0, -jnp.inf)
     for da in (0, 1, -1):
         gather_x.forward2(da)
-    gather_g.second(0)
+    gather_g.forward2(0)
     gather_x.forward2(2)
     for da in (1, -1, 2):
         gather_g.second(da)
@@ -475,9 +489,7 @@
             value = dot_nt(left[...], weights[at, :]).astype(BF)
             terms[:, pl.ds(pl.multiple_of((dy * RING + dz) * FEAT, 128), FEAT)] = value
 
-    project(0, 4)
-    gather_g.forward2(0)
-    project(4, 8)
+    project(0, 8)
     gather_g.forward2(1)
     pj[...] = qkv_ref[0:ROWS, :].astype(BF)
     head_forward(0)
@@ -523,13 +535,16 @@
     scatter_p.pass_on(3)
     head_backward(1)
     grad_q.send(2)
-    scatter_p.pass_on(0)
-    grad_o.send(0)
     grad_q.send(1)
     grad_q.add(2)
+    scatter_p.pass_on(0)
+    grad_q.send(3)
+    grad_o.ring.pass_on()
+    grad_q.add(1)
+    grad_o.send(0)
+    grad_q.add(3)
+    scatter_p.collect(2)
     grad_o.add(0)
-    grad_o.ring.pass_on()
-    scatter_p.collect(2)
     settle(gather_g.copies())
     make_terms(0, gp, wq, gf)
     scatter_b.send(2)
@@ -542,21 +557,18 @@
     make_terms(2, gp, wq, gf)
     scatter_b.send(0)
     scatter_p.collect(0)
-    grad_q.add(1)
-    grad_q.send(3)
     scatter_b.pass_on(2)
+    grad_q.send(0)
+    grad_q.ring.pass_on()
+    scatter_b.pass_on(1)
+    scatter_b.pass_on(3)
     for h in (0, 1):
         rows = pl.ds(h * HALF, HALF)
         live = lax.broadcasted_iota(jnp.int32, (HALF, FEAT), 0) + h * HALF < total_rows
         value = own_x[rows, :].astype(F32) + scatter_p.result(h)
         block_ref[rows, :] = jnp.where(live, value, 0.0).astype(BF)
     saved(pltpu.make_async_copy(block_ref, block_hbm, lsem.at[2]))
-    scatter_b.pass_on(1)
-    scatter_b.pass_on(3)
-    grad_q.add(3)
     scatter_b.pass_on(0)
-    grad_q.send(0)
-    grad_q.ring.pass_on()
     scatter_b.collect(2)
     grad_q.add(0)
     scatter_b.collect(1)
@@ -610,9 +622,7 @@
 def shards(
     patches, keep_index, keep_count, pack_dest, pack_offset, w_qkv, q_gain, k_gain, w_out, cotangent
 ):
-    vmem = pl.BlockSpec(memory_space=pltpu.VMEM)
     hbm = pl.BlockSpec(memory_space=pltpu.HBM)
-    smem = pl.BlockSpec(memory_space=pltpu.SMEM)
     results = (
         jax.ShapeDtypeStruct((ROWS, FEAT), BF),
         jax.ShapeDtypeStruct((ROWS, FEAT), BF),
@@ -622,9 +632,17 @@
     done = pl.pallas_call(
         kernel,
         out_shape=results,
-        in_specs=[smem] * 3 + [vmem] * 5 + [hbm] * 2,
+        in_specs=[hbm] * 10,
         out_specs=(hbm,) * 4,
         scratch_shapes=[
+            pltpu.SMEM((N_DP * N_DP,), jnp.int32),
+            pltpu.SMEM((N_DP * N_DP,), jnp.int32),
+            pltpu.SMEM((N_DP * N_DP,), jnp.int32),
+            pltpu.VMEM((N_DP, SLOTS), jnp.int32),
+            pltpu.VMEM((1, HEAD), F32),
+            pltpu.VMEM((1, HEAD), F32),
+            pltpu.VMEM((ROWS, FEAT), BF),
+            pltpu.VMEM((ROWS, FEAT), BF),
             *(pltpu.VMEM(r.shape, r.dtype) for r in results),
             pltpu.VMEM((D, QKV), BF),
             pltpu.VMEM((D, OUT), BF),
@@ -657,7 +675,7 @@
             pltpu.VMEM((3 * GRAD_ROWS, OUT), BF),
             pltpu.SemaphoreType.DMA((N_SEMS,)),
             pltpu.SemaphoreType.DMA((N_SEMS,)),
-            pltpu.SemaphoreType.DMA((6,)),
+            pltpu.SemaphoreType.DMA((14,)),
         ],
         compiler_params=pltpu.CompilerParams(
             collective_id=0, has_side_effects=True, vmem_limit_bytes=63 << 20

time: 140 us -> 132 us (0.943)
  Pallas kernels: 139 us -> 131 us
    pallas_call x1, Pallas kernels: 136 us -> 128 us  [shards(): pl.pallas_call(kernel, out_shape=results, in_specs=[hbm] * 10, out_specs=...]
where the time goes in v3:
time: 132 us
  Pallas kernels  131 us (99%)
    pallas_call x1, Pallas kernels, shards(): pl.pallas_call(kernel, out_shape=results, in_specs=[hbm] * 10, out_specs=...  128 us
    pallas_call x1, Pallas kernels, shards(): pl.pallas_call(hand_over, out_shape=results, in_specs=[hbm] * 4, out_spec...  3.43 us

profile of v3, /device:TPU:1, one launch (start us, length us, event | category | flops | bytes accessed | tf_op | source)
XLA Modules:
  0.0 132.2 jit_solution(6526291321944873586)
XLA Ops:
  0.6 127.9 %block.1 = (bf16[384,384]{1,0:T(8,128)(2,1)}, bf16[384,384]{1,0:T(8,128)(2,1)}, f32[768,768]{1,0:T(8,128)}, f32[768,256]{1,0:T(8,128)}) custom-call(s32[64]{0:T(128)} %count_hbm.1, s32[64]{0:T(128)} %dest_hbm.1, s32[64]{0:T(128)} %offset_hbm.1, s32[8,48]{1,0:T(8,128)} %keep_hbm.1, f32[1,128]{1,0:T(1,128)} %bitcast.2, f32[1,128]{1,0:T(1,128)} %bitcast.3, ...), custom_call_target="tpu_custom_call" | custom-call | flops 15000000512 | bytes 20000000 | tf_op jit(solution)/shard_map/block/pallas_call | solution.py:632
  128.6 3.4 %hand_over.1 = (bf16[384,384]{1,0:T(8,128)(2,1)}, bf16[384,384]{1,0:T(8,128)(2,1)}, f32[768,768]{1,0:T(8,128)}, f32[768,256]{1,0:T(8,128)}) custom-call(bf16[384,384]{1,0:T(8,128)(2,1)} %get-tuple-element.8.refs_0_, bf16[384,384]{1,0:T(8,128)(2,1)} %get-tuple-element.9.refs_1_, f32[768,768]{1,0:T(8,128)} %get-tuple-element.10.refs_2_, ...), custom_call_target="tpu_custom_call" | custom-call | tf_op jit(solution)/shard_map/hand_over/pallas_call | solution.py:689

commit v4 on v3

--- a/solution.py
+++ b/solution.py
@@ -273,9 +273,9 @@
             )
             self.order = []
 
-        def tile(self, dx, core, m):
+        def tile(self, dx, core):
             block = ((x + dx) % RING) * 2 + core
-            left = self.rows[:, pl.ds(pl.multiple_of(block * GRAD_ROWS + m * 256, 128), 256)]
+            left = self.rows[:, pl.ds(pl.multiple_of(block * GRAD_ROWS, 128), GRAD_ROWS)]
             return dot_tn(left, self.cols[...])
 
         def send(self, dx):
@@ -283,43 +283,45 @@
             if i >= self.slots:
                 self.swap[self.order[i - self.slots]].wait_send()
             self.order.append(dx)
-            slot = i % self.slots
-
-            @pl.loop(0, GRAD_ROWS // 256)
-            def _(m):
-                self.mine[slot, pl.ds(pl.multiple_of(m * 256, 256), 256), :] = self.tile(dx, 1 - c, m).astype(BF)
-
+            self.mine[i % self.slots] = self.tile(dx, 1 - c).astype(BF)
             self.swap[dx].start()
 
         def add(self, dx):
             self.swap[dx].wait_recv()
-
-            @pl.loop(0, GRAD_ROWS // 256)
-            def _(m):
-                at = pl.ds(pl.multiple_of(m * 256, 256), 256)
-                value = self.tile(dx, c, m) + self.theirs[dx, at, :].astype(F32)
-                if dx == 0:
-                    self.result[at, :] = value
-                else:
-                    self.theirs[dx, at, :] = value.astype(BF)
+            value = self.tile(dx, c) + self.theirs[dx].astype(F32)
+            if dx == 0:
+                self.result[...] = value
+            else:
+                self.theirs[dx] = value.astype(BF)
 
             if dx == 2:
                 self.ring.far()
             if dx == 3:
                 self.ring.near()
 
-        def finish(self):
-            self.ring.arrive()
-
-            @pl.loop(0, GRAD_ROWS // 64)
+        def gain(self, low, box_low, n=GRAD_ROWS // 2, step=64):
+            @pl.loop(0, n // step)
             def _(i):
-                low = pl.multiple_of(i * 64, 64)
-                at = pl.ds(low, 64)
-                self.result[at, :] = (
-                    self.result[at, :]
-                    + self.ring.box(GRAD_ROWS + low, 64)[...].astype(F32)
-                    + self.ring.box(2 * GRAD_ROWS + low, 64)[...].astype(F32)
-                )
+                more = pl.multiple_of(i * step, step)
+                at = pl.ds(low + more, step)
+                self.result[at, :] += self.ring.box(box_low + more, step)[...].astype(F32)
+
+        def begin_finish(self):
+            half = GRAD_ROWS // 2
+            self.ring.c2.wait_recv()
+            self.gain(half, GRAD_ROWS + half)
+            self.ring.c3.wait_recv()
+            self.gain(0, 2 * GRAD_ROWS)
+
+        def finish(self, target, sems):
+            half = GRAD_ROWS // 2
+            for copy, low, box_low, sem in (
+                (self.ring.c4, 0, GRAD_ROWS, sems[0]), (self.ring.c5, half, 2 * GRAD_ROWS + half, sems[1]),
+            ):
+                copy.wait_recv()
+                self.gain(low, box_low)
+                at = pl.ds(low, half)
+                saved(pltpu.make_async_copy(self.result.at[at], target.at[at], lsem.at[sem]))
 
         def close(self):
             for dx in self.order[-self.slots:]:
@@ -431,19 +433,9 @@
     gather_x.finish()
     load_q.wait()
 
-    def project(low, high):
-        @pl.loop(low, high)
-        def _(k):
-            at = pl.ds(pl.multiple_of(k * 768, 768), 768)
-            part = dot(xf[:, at], wq[at, :])
-
-            @pl.when(k == 0)
-            def _():
-                qkv_ref[0:ROWS, :] = part
-
-            @pl.when(k > 0)
-            def _():
-                qkv_ref[0:ROWS, :] += part
+    def project(n):
+        at = slice(n * 256, (n + 1) * 256)
+        pj[:, at] = dot(xf[...], wq[:, at]).astype(BF)
 
     def head_forward(h):
         base = h * 3 * HEAD
@@ -473,25 +465,29 @@
         gp[:, base + HEAD:base + 2 * HEAD] = head_norm_back(grad_kn, keys, key_inv, kg_ref[...]).astype(BF)
 
     def make_terms(group, left, weights, terms):
-        @pl.loop(0, (5, 4, 7)[group])
-        def _(i):
-            if group == 0:
-                late = i // 3
-                dy = (1 - late) * 2 + late * (2 * i - 5)
-                dz = (1 - late) * (i + 1) + late * 2
-            elif group == 1:
-                dy, dz = 1 + 2 * (i // 2), 1 + 2 * (i % 2)
-            else:
-                late = i // 4
-                dy, dz = late * (i - 3), (1 - late) * i
-            block = ((y + dy) % RING) * RING + (z + dz) % RING
-            at = pl.ds(pl.multiple_of(block * FEAT, 128), FEAT)
-            value = dot_nt(left[...], weights[at, :]).astype(BF)
-            terms[:, pl.ds(pl.multiple_of((dy * RING + dz) * FEAT, 128), FEAT)] = value
-
-    project(0, 8)
+        def some(places):
+            blocks = []
+            for dy, dz in places:
+                block = ((y + dy) % RING) * RING + (z + dz) % RING
+                blocks.append(weights[pl.ds(pl.multiple_of(block * FEAT, 128), FEAT), :])
+            value = dot_nt(left[...], jnp.concatenate(blocks, axis=0)).astype(BF)
+            for i, (dy, dz) in enumerate(places):
+                terms[:, pl.ds((dy * RING + dz) * FEAT, FEAT)] = value[:, i * FEAT:(i + 1) * FEAT]
+
+        if group == 0:
+            some([(2, 1), (2, 2), (2, 3)])
+            some([(1, 2), (3, 2)])
+        elif group == 1:
+            some([(1, 1), (1, 3)])
+            some([(3, 1), (3, 3)])
+        else:
+            some([(0, 1), (0, 2), (0, 3)])
+            some([(1, 0), (2, 0), (3, 0), (0, 0)])
+
+    project(0)
+    project(1)
     gather_g.forward2(1)
-    pj[...] = qkv_ref[0:ROWS, :].astype(BF)
+    project(2)
     head_forward(0)
     gather_g.forward2(-1)
     head_forward(1)
@@ -507,42 +503,29 @@
     gather_g.finish()
 
     def grad_attended():
-        @pl.loop(0, 8)
-        def _(k):
-            at = pl.ds(pl.multiple_of(k * 768, 768), 768)
-            part = dot(gf[:, at], wo[at, :])
-
-            @pl.when(k == 0)
-            def _():
-                qkv_ref[0:ROWS, 0:OUT] = part
-
-            @pl.when(k > 0)
-            def _():
-                qkv_ref[0:ROWS, 0:OUT] += part
-
-        ga[...] = qkv_ref[0:ROWS, 0:OUT].astype(BF)
+        ga[...] = dot(gf[...], wo[...]).astype(BF)
 
     grad_o.send(2)
     grad_o.send(1)
+    grad_o.send(3)
+    grad_attended()
     grad_o.add(2)
-    scatter_p.pass_on(2)
-    grad_attended()
-    grad_o.send(3)
     grad_o.add(1)
     grad_o.add(3)
-    scatter_p.pass_on(1)
+    scatter_p.pass_on(2)
     head_backward(0)
-    scatter_p.pass_on(3)
     head_backward(1)
     grad_q.send(2)
     grad_q.send(1)
+    scatter_p.pass_on(1)
     grad_q.add(2)
-    scatter_p.pass_on(0)
     grad_q.send(3)
     grad_o.ring.pass_on()
     grad_q.add(1)
+    scatter_p.pass_on(3)
+    grad_q.add(3)
+    scatter_p.pass_on(0)
     grad_o.send(0)
-    grad_q.add(3)
     scatter_p.collect(2)
     grad_o.add(0)
     settle(gather_g.copies())
@@ -558,23 +541,23 @@
     scatter_b.send(0)
     scatter_p.collect(0)
     scatter_b.pass_on(2)
-    grad_q.send(0)
-    grad_q.ring.pass_on()
-    scatter_b.pass_on(1)
-    scatter_b.pass_on(3)
     for h in (0, 1):
         rows = pl.ds(h * HALF, HALF)
         live = lax.broadcasted_iota(jnp.int32, (HALF, FEAT), 0) + h * HALF < total_rows
         value = own_x[rows, :].astype(F32) + scatter_p.result(h)
         block_ref[rows, :] = jnp.where(live, value, 0.0).astype(BF)
     saved(pltpu.make_async_copy(block_ref, block_hbm, lsem.at[2]))
+    grad_q.ring.pass_on()
+    scatter_b.pass_on(1)
+    grad_q.send(0)
+    scatter_b.pass_on(3)
+    grad_o.begin_finish()
+    grad_o.finish(out_hbm, (3, 14))
     scatter_b.pass_on(0)
     scatter_b.collect(2)
     grad_q.add(0)
     scatter_b.collect(1)
     scatter_b.collect(3)
-    grad_o.finish()
-    saved(pltpu.make_async_copy(out_ref, out_hbm, lsem.at[3]))
     scatter_b.last_pass()
     scatter_b.collect(0)
     for h in (0, 1):
@@ -584,12 +567,12 @@
     for copy in swap_g:
         start(copy)
     ar2[here, :] = og2[here, :]
-    grad_q.finish()
-    saved(pltpu.make_async_copy(qkv_ref, qkv_hbm, lsem.at[4]))
+    grad_q.begin_finish()
     for copy in swap_g:
         copy.wait_recv()
     pgrad_ref[...] = dot(sel_t[...], ar2[...]).astype(BF)
     saved(pltpu.make_async_copy(pgrad_ref, pgrad_hbm, lsem.at[5]))
+    grad_q.finish(qkv_hbm, (4, 15))
     grad_q.close()
     grad_o.close()
     settle(list(sent.values()))
@@ -675,7 +658,7 @@
             pltpu.VMEM((3 * GRAD_ROWS, OUT), BF),
             pltpu.SemaphoreType.DMA((N_SEMS,)),
             pltpu.SemaphoreType.DMA((N_SEMS,)),
-            pltpu.SemaphoreType.DMA((14,)),
+            pltpu.SemaphoreType.DMA((16,)),
         ],
         compiler_params=pltpu.CompilerParams(
             collective_id=0, has_side_effects=True, vmem_limit_bytes=63 << 20

time: 132 us -> 129 us (0.977)
  Pallas kernels: 131 us -> 128 us
    pallas_call x1, Pallas kernels: 128 us -> 125 us  [shards(): pl.pallas_call(kernel, out_shape=results, in_specs=[hbm] * 10, out_specs=...]
where the time goes in v4:
time: 129 us
  Pallas kernels  128 us (99%)
    pallas_call x1, Pallas kernels, shards(): pl.pallas_call(kernel, out_shape=results, in_specs=[hbm] * 10, out_specs=...  125 us
    pallas_call x1, Pallas kernels, shards(): pl.pallas_call(hand_over, out_shape=results, in_specs=[hbm] * 4, out_spec...  3.43 us

profile of v4, /device:TPU:1, one launch (start us, length us, event | category | flops | bytes accessed | tf_op | source)
XLA Modules:
  0.0 128.9 jit_solution(6697247480319190667)
XLA Ops:
  0.6 124.6 %block.1 = (bf16[384,384]{1,0:T(8,128)(2,1)}, bf16[384,384]{1,0:T(8,128)(2,1)}, f32[768,768]{1,0:T(8,128)}, f32[768,256]{1,0:T(8,128)}) custom-call(s32[64]{0:T(128)} %count_hbm.1, s32[64]{0:T(128)} %dest_hbm.1, s32[64]{0:T(128)} %offset_hbm.1, s32[8,48]{1,0:T(8,128)} %keep_hbm.1, f32[1,128]{1,0:T(1,128)} %bitcast.2, f32[1,128]{1,0:T(1,128)} %bitcast.3, ...), custom_call_target="tpu_custom_call" | custom-call | flops 15000000512 | bytes 20000000 | tf_op jit(solution)/shard_map/block/pallas_call | solution.py:615
  125.3 3.4 %hand_over.1 = (bf16[384,384]{1,0:T(8,128)(2,1)}, bf16[384,384]{1,0:T(8,128)(2,1)}, f32[768,768]{1,0:T(8,128)}, f32[768,256]{1,0:T(8,128)}) custom-call(bf16[384,384]{1,0:T(8,128)(2,1)} %get-tuple-element.8.refs_0_, bf16[384,384]{1,0:T(8,128)(2,1)} %get-tuple-element.9.refs_1_, f32[768,768]{1,0:T(8,128)} %get-tuple-element.10.refs_2_, ...), custom_call_target="tpu_custom_call" | custom-call | tf_op jit(solution)/shard_map/hand_over/pallas_call | solution.py:672

commit v5 on v4

--- a/solution.py
+++ b/solution.py
@@ -510,15 +510,15 @@
     grad_o.send(3)
     grad_attended()
     grad_o.add(2)
+    head_backward(0)
+    head_backward(1)
+    grad_q.send(2)
     grad_o.add(1)
     grad_o.add(3)
     scatter_p.pass_on(2)
-    head_backward(0)
-    head_backward(1)
-    grad_q.send(2)
     grad_q.send(1)
+    grad_q.add(2)
     scatter_p.pass_on(1)
-    grad_q.add(2)
     grad_q.send(3)
     grad_o.ring.pass_on()
     grad_q.add(1)
@@ -568,11 +568,11 @@
         start(copy)
     ar2[here, :] = og2[here, :]
     grad_q.begin_finish()
+    grad_q.finish(qkv_hbm, (4, 15))
     for copy in swap_g:
         copy.wait_recv()
     pgrad_ref[...] = dot(sel_t[...], ar2[...]).astype(BF)
     saved(pltpu.make_async_copy(pgrad_ref, pgrad_hbm, lsem.at[5]))
-    grad_q.finish(qkv_hbm, (4, 15))
     grad_q.close()
     grad_o.close()
     settle(list(sent.values()))
@@ -584,7 +584,7 @@
     inputs, outputs, held, sems = refs[:4], refs[4:8], refs[8:12], refs[12]
     pairs = []
     for source, target, stage in zip(inputs, outputs, held):
-        pieces = max(1, source.shape[0] * source.shape[1] // (192 * 768))
+        pieces = max(1, source.shape[0] * source.shape[1] // (384 * 768))
         step = source.shape[0] // pieces
         for p in range(pieces):
             at = pl.ds(p * step, step)

time: 129 us -> 128 us (level)
  no operation moved by 1% of the time
where the time goes in v5:
time: 128 us
  Pallas kernels  127 us (99%)
    pallas_call x1, Pallas kernels, shards(): pl.pallas_call(kernel, out_shape=results, in_specs=[hbm] * 10, out_specs=...  124 us
    pallas_call x1, Pallas kernels, shards(): pl.pallas_call(hand_over, out_shape=results, in_specs=[hbm] * 4, out_spec...  3.26 us

profile of v5, /device:TPU:1, one launch (start us, length us, event | category | flops | bytes accessed | tf_op | source)
XLA Modules:
  0.0 127.9 jit_solution(2703448924142166459)
XLA Ops:
  0.6 123.8 %block.1 = (bf16[384,384]{1,0:T(8,128)(2,1)}, bf16[384,384]{1,0:T(8,128)(2,1)}, f32[768,768]{1,0:T(8,128)}, f32[768,256]{1,0:T(8,128)}) custom-call(s32[64]{0:T(128)} %count_hbm.1, s32[64]{0:T(128)} %dest_hbm.1, s32[64]{0:T(128)} %offset_hbm.1, s32[8,48]{1,0:T(8,128)} %keep_hbm.1, f32[1,128]{1,0:T(1,128)} %bitcast.2, f32[1,128]{1,0:T(1,128)} %bitcast.3, ...), custom_call_target="tpu_custom_call" | custom-call | flops 15000000512 | bytes 20000000 | tf_op jit(solution)/shard_map/block/pallas_call | solution.py:615
  124.5 3.3 %hand_over.1 = (bf16[384,384]{1,0:T(8,128)(2,1)}, bf16[384,384]{1,0:T(8,128)(2,1)}, f32[768,768]{1,0:T(8,128)}, f32[768,256]{1,0:T(8,128)}) custom-call(bf16[384,384]{1,0:T(8,128)(2,1)} %get-tuple-element.8.refs_0_, bf16[384,384]{1,0:T(8,128)(2,1)} %get-tuple-element.9.refs_1_, f32[768,768]{1,0:T(8,128)} %get-tuple-element.10.refs_2_, ...), custom_call_target="tpu_custom_call" | custom-call | tf_op jit(solution)/shard_map/hand_over/pallas_call | solution.py:672
